TPU v7x, 32 devices: a whole 2x2x4 slice. The times are simulated.
32 devices in a mesh: shard: 2 (over y), replica: 16 (over z, x, core).
Axes of the slice: x: 2, y: 2, z: 4, core: 2. Of those that a mesh axis runs over, the one named last changes fastest.
Arguments:
- tokens: bfloat16 [32768, 1024], P(('shard', 'replica')), may hold values from -6 to 6
- cotangent: bfloat16 [32768, 1024], P(('shard', 'replica')), may hold values from -6 to 6
- segment_ids: int32 [32, 1024], P(('shard', 'replica')), may hold values from 0 to 3, never falling along the last dimension, each value on 1 to 800 neighbouring positions
- owners: int32 [96], replicated, may hold values from 0 to 15, as said below
- master: float32 [192, 1024, 128], P('replica', 'shard'), may hold values from -4 to 4
- moment_one: float32 [192, 1024, 128], P('replica', 'shard'), may hold values from -6553.6 to 6553.6
- moment_two: float32 [192, 1024, 128], P('replica', 'shard'), may hold values from 2.62144 to 42.5984
- vectors: float32 [12, 1024], replicated, may hold values from -2 to 2
- vector_one: float32 [12, 1024], replicated, may hold values from -13107.2 to 13107.2
- vector_two: float32 [12, 1024], replicated, may hold values from 8.192 to 131.072
Outputs:
- output: bfloat16 [32768, 1024], P(('shard', 'replica'))
- input_grad: bfloat16 [32768, 1024], P(('shard', 'replica'))
- new_master: float32 [192, 1024, 128], P('replica', 'shard')
- master_copy: bfloat16 [192, 1024, 128], P('replica', 'shard')
- new_one: float32 [192, 1024, 128], P('replica', 'shard')
- new_two: float32 [192, 1024, 128], P('replica', 'shard')
- new_vectors: float32 [12, 1024], replicated
- new_vector_one: float32 [12, 1024], replicated
- new_vector_two: float32 [12, 1024], replicated
Inputs may be any that keep to these rules, and one draw needn't show every extreme that they name: owners[j] is the replica that keeps stripe j. One replica keeps exactly 12 stripes; every other keeps at most 12, and the counts of the others differ by at most one. A replica keeps its stripes in its slots in increasing stripe order; its later slots are unused. `segment_ids`: within each sequence segment numbers never fall and each document has 1 to 800 tokens, one exactly 800.
All inputs are finite; a program needn't handle non-finite values.
Results may differ from a plain program's by a relative error of at most 0.018.
Values may be sent and summed in bfloat16 or wider, within the bound.
No kernel may reach another device: no remote copies, remote signals or barrier semaphores. Data moves between devices by JAX's collectives and lax.ppermute only.
A program may use at most 320 MiB of HBM per device.

v0:
```python
import jax
import jax.numpy as jnp
from jax import lax
from jax.sharding import PartitionSpec as P

D = 1024
HEADS = 16
HEAD_DIM = 64
FF = 4096
STEP = 10


beta_one = 0.9
beta_two = 0.999
epsilon = 1e-08
rate_matrix = 0.05
rate_vector = 0.3
decay_rate = 0.01


def layer_norm(hidden, gain, shift):
    centered = hidden - jnp.mean(hidden, axis=-1, keepdims=True)
    spread = jnp.mean(centered * centered, axis=-1, keepdims=True)
    return centered * lax.rsqrt(spread + 1e-05) * gain + shift


def exact_gelu(values):
    return jax.nn.gelu(values, approximate=False)


def adamw(param, first, second, grad, rate, decay):
    first = beta_one * first + (1.0 - beta_one) * grad
    second = beta_two * second + (1.0 - beta_two) * grad * grad
    corrected = (
        first / (1.0 - beta_one**STEP) / (jnp.sqrt(second / (1.0 - beta_two**STEP)) + epsilon)
    )
    return (param - rate * (corrected + decay * param), first, second)


def attend_block(query_part, key_part, value_part, same):
    scale = HEAD_DIM ** (-0.5)
    raw = (
        jnp.einsum("qhd,khd->hqk", query_part, key_part, preferred_element_type=jnp.float32) * scale
    )
    masked = jnp.where(same[None], raw, -1e30)
    top = jnp.max(masked, axis=-1, keepdims=True)
    expd = jnp.exp(masked - top)
    total = jnp.sum(expd, axis=-1, keepdims=True)
    probs = (expd / total).astype(jnp.bfloat16)
    context = jnp.einsum("hqk,khd->qhd", probs, value_part, preferred_element_type=jnp.float32)
    return (context, top + jnp.log(total))


def attend_back(query_part, key_part, value_part, same, log_total, grad_context):
    scale = HEAD_DIM ** (-0.5)
    raw = (
        jnp.einsum("qhd,khd->hqk", query_part, key_part, preferred_element_type=jnp.float32) * scale
    )
    masked = jnp.where(same[None], raw, -1e30)
    probs = jnp.exp(masked - log_total)
    probs_low = probs.astype(jnp.bfloat16)
    grad_value = jnp.einsum(
        "hqk,qhd->khd", probs_low, grad_context, preferred_element_type=jnp.float32
    )
    grad_probs = jnp.einsum(
        "qhd,khd->hqk", grad_context, value_part, preferred_element_type=jnp.float32
    )
    inner = jnp.sum(grad_probs * probs, axis=-1, keepdims=True)
    grad_scores = (probs * (grad_probs - inner)).astype(jnp.bfloat16)
    grad_query = (
        jnp.einsum("hqk,khd->qhd", grad_scores, key_part, preferred_element_type=jnp.float32)
        * scale
    )
    grad_key = (
        jnp.einsum("hqk,qhd->khd", grad_scores, query_part, preferred_element_type=jnp.float32)
        * scale
    )
    return (grad_query, grad_key, grad_value)


def on_device(
    tokens,
    cotangent,
    segment_ids,
    owners,
    master,
    moment_one,
    moment_two,
    vectors,
    vector_one,
    vector_two,
):
    replica_count = lax.axis_size("replica")
    replica_index = lax.axis_index("replica")
    shard_count = lax.axis_size("shard")
    slot_count, shard_rows, stripe = master.shape
    columns = 4 * D + 2 * FF
    stripe_count = columns // stripe
    stripe_ids = jnp.arange(stripe_count, dtype=jnp.int32)
    earlier = (owners[None, :] == owners[:, None]) & (stripe_ids[None, :] < stripe_ids[:, None])
    slot_of = jnp.sum(earlier.astype(jnp.int32), axis=1)
    slot_place = owners * slot_count + slot_of
    halves = master.astype(jnp.bfloat16)
    gathered = lax.all_gather(halves, ("shard", "replica"), axis=0, tiled=True)
    grouped = gathered.reshape(shard_count, replica_count * slot_count, shard_rows, stripe)
    picked = jnp.take(grouped, slot_place, axis=1)
    weights = picked.transpose(0, 2, 1, 3).reshape(shard_count * shard_rows, columns)
    w_qkv = weights[:, : 3 * D]
    w_out = weights[:, 3 * D : 4 * D]
    w_up = weights[:, 4 * D : 4 * D + FF]
    w_down = weights[:, 4 * D + FF :]
    up_bias = vectors[8:].reshape(FF)
    sequences, length = segment_ids.shape
    row_count = tokens.shape[0]
    query_block = min(512, length)
    head_group = min(4, HEADS)
    transposed = (((1,), (1,)), ((), ()))
    over_rows = (((0,), (0,)), ((), ()))
    projected = jnp.dot(tokens, w_qkv, preferred_element_type=jnp.float32)
    query = (projected[:, :D] + vectors[0]).astype(jnp.bfloat16)
    keys = projected[:, D : 2 * D].astype(jnp.bfloat16)
    values = (projected[:, 2 * D :] + vectors[1]).astype(jnp.bfloat16)
    shape_four = (sequences, length, HEADS, HEAD_DIM)
    query_four = query.reshape(shape_four)
    key_four = keys.reshape(shape_four)
    value_four = values.reshape(shape_four)
    saved = {}
    context_rows = []
    seq_pos = 0
    same_all = segment_ids[seq_pos][:, None] == segment_ids[seq_pos][None, :]
    for block_pos in range(length // query_block):
        first_row = block_pos * query_block
        pieces = []
        for head_pos in range(0, HEADS, head_group):
            context_part, log_total = attend_block(
                query_four[
                    seq_pos, first_row : first_row + query_block, head_pos : head_pos + head_group
                ],
                key_four[seq_pos, :, head_pos : head_pos + head_group],
                value_four[seq_pos, :, head_pos : head_pos + head_group],
                same_all[first_row : first_row + query_block],
            )
            saved[seq_pos, block_pos, head_pos] = log_total
            pieces.append(context_part)
        context_rows.append(jnp.concatenate(pieces, axis=1))
    context = jnp.concatenate(context_rows, axis=0).reshape(row_count, D).astype(jnp.bfloat16)
    attn = jnp.dot(context, w_out, preferred_element_type=jnp.float32) + vectors[2]
    first_sum = tokens.astype(jnp.float32) + attn
    normed, first_back = jax.vjp(layer_norm, first_sum, vectors[3], vectors[4])
    normed_low = normed.astype(jnp.bfloat16)
    upward = jnp.dot(normed_low, w_up, preferred_element_type=jnp.float32) + up_bias
    active_full, gelu_back = jax.vjp(exact_gelu, upward)
    active = active_full.astype(jnp.bfloat16)
    branch = (
        lax.dot_general(active, w_down, transposed, preferred_element_type=jnp.float32) + vectors[5]
    )
    output, second_back = jax.vjp(layer_norm, normed + branch, vectors[6], vectors[7])
    grad_second, grad_gain_two, grad_shift_two = second_back(cotangent.astype(jnp.float32))
    grad_branch = grad_second.astype(jnp.bfloat16)
    grad_active = jnp.dot(grad_branch, w_down, preferred_element_type=jnp.float32)
    grad_up = gelu_back(grad_active)[0].astype(jnp.bfloat16)
    grad_normed = grad_second + lax.dot_general(
        grad_up, w_up, transposed, preferred_element_type=jnp.float32
    )
    grad_first, grad_gain_one, grad_shift_one = first_back(grad_normed)
    grad_attn = grad_first.astype(jnp.bfloat16)
    grad_context = lax.dot_general(
        grad_attn, w_out, transposed, preferred_element_type=jnp.float32
    ).astype(jnp.bfloat16)
    grad_context_four = grad_context.reshape(shape_four)
    seq_pos = 0
    same_all = segment_ids[seq_pos][:, None] == segment_ids[seq_pos][None, :]
    query_heads = []
    key_heads = []
    value_heads = []
    for head_pos in range(0, HEADS, head_group):
        key_total = jnp.zeros((length, head_group, HEAD_DIM), jnp.float32)
        value_total = jnp.zeros((length, head_group, HEAD_DIM), jnp.float32)
        query_parts = []
        for block_pos in range(length // query_block):
            first_row = block_pos * query_block
            grad_query_part, grad_key_part, grad_value_part = attend_back(
                query_four[
                    seq_pos, first_row : first_row + query_block, head_pos : head_pos + head_group
                ],
                key_four[seq_pos, :, head_pos : head_pos + head_group],
                value_four[seq_pos, :, head_pos : head_pos + head_group],
                same_all[first_row : first_row + query_block],
                saved[seq_pos, block_pos, head_pos],
                grad_context_four[
                    seq_pos, first_row : first_row + query_block, head_pos : head_pos + head_group
                ],
            )
            query_parts.append(grad_query_part)
            key_total = key_total + grad_key_part
            value_total = value_total + grad_value_part
        query_heads.append(jnp.concatenate(query_parts, axis=0))
        key_heads.append(key_total)
        value_heads.append(value_total)
    query_seqs = jnp.concatenate(query_heads, axis=1)
    key_seqs = jnp.concatenate(key_heads, axis=1)
    value_seqs = jnp.concatenate(value_heads, axis=1)
    grad_query = query_seqs.reshape(row_count, D).astype(jnp.bfloat16)
    grad_key = key_seqs.reshape(row_count, D).astype(jnp.bfloat16)
    grad_value = value_seqs.reshape(row_count, D).astype(jnp.bfloat16)
    grad_projected = jnp.concatenate([grad_query, grad_key, grad_value], axis=1)
    input_grad = grad_first + lax.dot_general(
        grad_projected, w_qkv, transposed, preferred_element_type=jnp.float32
    )
    slot_range = jnp.arange(slot_count, dtype=jnp.int32)
    matches = (
        (owners[None, :] == replica_index) & (slot_of[None, :] == slot_range[:, None])
    ).astype(jnp.int32)
    stripe_pick = jnp.sum(matches * stripe_ids[None, :], axis=1)
    keep = (jnp.sum(matches, axis=1) > 0)[:, None, None]
    part_qkv = lax.dot_general(
        tokens, grad_projected, over_rows, preferred_element_type=jnp.float32
    )
    part_out = lax.dot_general(context, grad_attn, over_rows, preferred_element_type=jnp.float32)
    part_up = lax.dot_general(normed_low, grad_up, over_rows, preferred_element_type=jnp.float32)
    part_down = lax.dot_general(grad_branch, active, over_rows, preferred_element_type=jnp.float32)
    grad_shard = lax.psum_scatter(
        jnp.concatenate([part_qkv, part_out, part_up, part_down], axis=1).astype(jnp.bfloat16),
        "shard",
        scatter_dimension=0,
        tiled=True,
    )
    summed = lax.psum(grad_shard, "replica").astype(jnp.float32)
    stripes = summed.reshape(shard_rows, stripe_count, stripe)
    slot_grad = jnp.take(stripes, stripe_pick, axis=1).transpose(1, 0, 2)
    vector_terms = jnp.stack(
        [
            jnp.sum(grad_query.astype(jnp.float32), axis=0),
            jnp.sum(grad_value.astype(jnp.float32), axis=0),
            jnp.sum(grad_attn.astype(jnp.float32), axis=0),
            grad_gain_one,
            grad_shift_one,
            jnp.sum(grad_branch.astype(jnp.float32), axis=0),
            grad_gain_two,
            grad_shift_two,
        ]
    )
    up_terms = jnp.sum(grad_up.astype(jnp.float32), axis=0).reshape(FF // D, D)
    vector_grad = lax.psum(jnp.concatenate([vector_terms, up_terms], axis=0), ("shard", "replica"))
    new_master, new_one, new_two = adamw(
        master, moment_one, moment_two, slot_grad, rate_matrix, decay_rate
    )
    new_master = jnp.where(keep, new_master, 0.0)
    new_one = jnp.where(keep, new_one, 0.0)
    new_two = jnp.where(keep, new_two, 0.0)
    new_vectors, new_vector_one, new_vector_two = adamw(
        vectors, vector_one, vector_two, vector_grad, rate_vector, 0.0
    )
    return (
        output.astype(jnp.bfloat16),
        input_grad.astype(jnp.bfloat16),
        new_master,
        new_master.astype(jnp.bfloat16),
        new_one,
        new_two,
        new_vectors,
        new_vector_one,
        new_vector_two,
    )


def solution(mesh):
    return jax.shard_map(
        on_device,
        mesh=mesh,
        in_specs=(
            P(("shard", "replica"), None),
            P(("shard", "replica"), None),
            P(("shard", "replica"), None),
            P(),
            P("replica", "shard", None),
            P("replica", "shard", None),
            P("replica", "shard", None),
            P(),
            P(),
            P(),
        ),
        out_specs=(
            P(("shard", "replica"), None),
            P(("shard", "replica"), None),
            P("replica", "shard", None),
            P("replica", "shard", None),
            P("replica", "shard", None),
            P("replica", "shard", None),
            P(),
            P(),
            P(),
        ),
        check_vma=False,
    )
```

profile of v0, /device:TPU:0, one launch (start us, length us, event | category | flops | bytes accessed | tf_op | source)
XLA Modules:
  0.0 1401.4 jit_solution(7596146304049508560)
XLA Ops:
  7.2 3.5 convert_element_type.164
  11.4 2.6 copy.68
  14.0 3.9 copy.66
  19.9 269.8 %all-gather.2.cloned.1.call-done = bf16[384,512,128]{2,1,0:T(8,128)(2,1)} async-done(((bf16[12,512,128]{2,1,0:T(8,128)(2,1)}), bf16[384,512,128]{2,1,0:T(8,128)(2,1)}) %all-gather.2.cloned.1.call-update) | async-done | bytes 50331664 | tf_op jit(solution)/shard_map/all_gather | solution.py:104
  289.8 17.4 %gather_fusion = bf16[96,2,512,128]{3,2,1,0:T(8,128)(2,1)} fusion(bf16[2,192,512,128]{3,2,1,0:T(8,128)(2,1)} %bitcast.389, s32[1024]{0:T(1024)S(1)} %pad_clamp_fusion.1), kind=kCustom, calls=%fused_computation | custom fusion | bytes 50332032 | tf_op jit(solution)/shard_map/jit(_take)/gather | solution.py:106
  307.2 12.6 select_bitcast_fusion
  319.8 60.9 %copy.67 = bf16[2,512,96,128]{3,2,1,0:T(8,128)(2,1)} copy(bf16[2,512,96,128]{3,1,0,2:T(8,128)(2,1)S(1)} %select_bitcast_fusion) | data formatting | bytes 50331648 | tf_op jit(solution)/shard_map/jit(_take)/select_n | solution.py:106
  380.7 18.1 %copy.83 = bf16[128,8,96,128]{3,1,2,0:T(8,128)(2,1)S(1)} copy(bf16[128,8,96,128]{3,2,1,0:T(8,128)(2,1)} %bitcast.327) | data formatting | bytes 50331648
  398.8 10.4 convolution_bitcast_fusion
  413.6 4.6 fusion.56
  477.6 4.4 fusion.180
  483.4 48.3 %multiply_convert_fusion = (bf16[1024,4096]{1,0:T(8,128)(2,1)}, f32[1024,4096]{1,0:T(8,128)}, f32[1024,4096]{1,0:T(8,128)}) fusion(f32[4096]{0:T(1024)S(1)} %bitcast.433, bf16[1024,12288]{1,0:T(8,128)(2,1)} %bitcast.335, bf16[1024,1024]{0,1:T(8,128)(2,1)S(1)} %fusion.164.clone.5), kind=kOutput, calls=%fused_computation.9 | convolution fusion | flops 8866758656 | bytes 52445184 | tf_op jit(solution)/shard_map/dot_general | solution.py:151
  531.8 14.4 %fusion.181 = (f32[1024]{0:T(1024)S(1)}, f32[1024,1024]{0,1:T(8,128)S(1)}) fusion(f32[1024]{0:T(1024)S(1)} %bitcast.438, bf16[1024,4096]{1,0:T(8,128)(2,1)} %get-tuple-element.88, bf16[1024,12288]{1,0:T(8,128)(2,1)} %bitcast.336, f32[1024]{0:T(1024)S(1)} %bitcast.428, f32[1024]{0:T(1024)S(1)} %bitcast.419, f32[1024]{0:T(1024)S(1)} %fusion.158, ...), kind=kOutput, calls=%fused_computation.322 | convolution fusion | flops 8597273600 | bytes 25190400 | tf_op jit(solution)/shard_map/dot_general | solution.py:155
  548.2 3.3 fusion.38
  551.5 3.9 convert_reduce_fusion.2
  555.4 11.2 convolution_convert_fusion
  566.6 25.3 %convert_reduce_fusion = (f32[4096]{0:T(1024)}, bf16[1024,4096]{1,0:T(8,128)(2,1)}) fusion(f32[1024,4096]{1,0:T(8,128)} %get-tuple-element.89, bf16[1024,1024]{0,1:T(8,128)(2,1)} %copy-done.38, bf16[1024,12288]{1,0:T(8,128)(2,1)} %bitcast.337, f32[1024,4096]{1,0:T(8,128)} %get-tuple-element.128, f32[4096]{0:T(1024)S(1)} %bitcast.434), kind=kOutput, calls=%fused_computation.7 | convolution fusion | flops 8661233664 | bytes 52461568 | tf_op jit(solution)/shard_map/dot_general | solution.py:160
  591.9 18.2 %multiply_reduce_fusion.8 = (f32[1024]{0:T(1024)}, f32[1024]{0:T(1024)S(1)}, f32[1024]{0:T(1024)}, f32[1024,1024]{0,1:T(8,128)}) fusion(f32[1024,1024]{0,1:T(8,128)S(1)} %get-tuple-element.127, f32[1024]{0:T(1024)S(1)} %fusion.158, f32[1024]{0:T(1024)S(1)} %broadcast_multiply_fusion.1, f32[1024]{0:T(1024)S(1)} %bitcast.420, ...), kind=kOutput, calls=%fused_computation.129 | convolution fusion | flops 8607757312 | bytes 31502336 | tf_op jit(solution)/shard_map/dot_general | solution.py:162
  610.1 15.2 %convolution_convert_fusion.1 = bf16[1024,4096]{1,0:T(8,128)(2,1)} fusion(bf16[1024,4096]{1,0:T(8,128)(2,1)} %get-tuple-element.149, f32[1024,1024]{0,1:T(8,128)S(1)} %get-tuple-element.127, f32[1024]{0:T(1024)S(1)} %bitcast.429, f32[1024]{0:T(1024)S(1)} %bitcast.421, f32[1024]{0:T(1024)S(1)} %fusion.158, f32[1024]{0:T(1024)S(1)} %broadcast_multiply_fusion.1), kind=kOutput, calls=%fused_computation.72 | convolution fusion | flops 8599371776 | bytes 20987904 | tf_op jit(solution)/shard_map/dot_general | solution.py:220
  629.6 3.7 convolution_convert_fusion.3
  633.4 3.9 convolution_convert_fusion.2
  639.9 4.4 multiply_reduce_fusion
  644.3 2.6 multiply_reduce_fusion.1
  648.9 3.2 fusion.125
  654.0 3.6 fusion.43
  657.5 6.5 multiply_reduce_fusion.2
  664.1 3.4 multiply_reduce_fusion.3
  669.3 3.1 fusion.123
  672.5 2.9 fusion.153
  675.4 3.6 fusion.47
  678.9 6.5 multiply_reduce_fusion.4
  685.5 3.9 multiply_reduce_fusion.5
  691.2 3.2 fusion.121
  694.4 2.9 fusion.152
  699.8 4.4 multiply_reduce_fusion.6
  704.2 2.6 multiply_reduce_fusion.7
  708.6 3.1 fusion.119
  711.7 2.8 fusion.151
  714.5 4.1 copy.72
  718.7 6.1 fusion.108
  724.7 6.6 fusion.102
  731.4 3.4 fusion.96
  734.8 3.4 fusion.90
  740.0 3.8 fusion.126
  743.8 2.6 fusion.115
  746.5 4.5 multiply_convert_fusion.3
  751.0 3.2 fusion.124
  758.1 2.9 fusion.122
  762.9 4.4 multiply_convert_fusion.7
  773.3 2.7 convert_reduce_fusion.5
  777.3 13.9 convert_bitcast_fusion
  791.2 9.0 copy.71
  800.2 16.7 %pad_maximum_fusion = bf16[1024,12288]{1,0:T(8,128)(2,1)} fusion(bf16[1024,4096]{1,0:T(8,128)(2,1)} %convolution_convert_fusion, bf16[1024,4096]{1,0:T(8,128)(2,1)} %convolution_convert_fusion.1, bf16[1024,1024]{1,0:T(8,128)(2,1)S(1)} %copy-done.23, bf16[1024,3072]{1,0:T(8,128)(2,1)} %copy.71), kind=kLoop, calls=%fused_computation.3 | loop fusion | flops 100663296 | bytes 50331648 | tf_op jit(solution)/shard_map/concatenate | solution.py:223
  817.0 277.6 %reduce-scatter.4.cloned.1.call-done = bf16[512,12288]{1,0:T(8,128)(2,1)} async-done(((bf16[1024,12288]{1,0:T(8,128)(2,1)}), bf16[512,12288]{1,0:T(8,128)(2,1)}) %reduce-scatter.4.cloned.1.call-update) | async-done | bytes 12582928
  1094.6 16.6 %copy.73 = bf16[512,12288]{0,1:T(8,128)(2,1)} copy(bf16[512,12288]{1,0:T(8,128)(2,1)} %reduce-scatter.4.cloned.1.call-done) | data formatting | bytes 25165824 | tf_op jit(solution)/shard_map/reduce_scatter | solution.py:222
  1111.2 16.6 %copy.74 = bf16[512,96,128]{2,0,1:T(8,128)(2,1)} copy(bf16[512,96,128]{0,2,1:T(8,128)(2,1)} %bitcast.328) | data formatting | bytes 25165824 | tf_op jit(solution)/shard_map/reshape | solution.py:229
  1129.4 2.5 copy.75
  1132.1 12.0 add_convert_fusion.1
  1144.3 2.6 copy.76
  1147.0 41.2 %psum.15 = f32[12,1024]{1,0:T(8,128)S(1)} all-reduce(f32[12,1024]{1,0:T(8,128)S(1)} %concatenate.56), channel_id=1, replica_groups=mesh['shard'=2,'replica'=16] {'shard','replica'}, use_global_device_ids=true, to_apply=%region_46.47 | all-reduce | flops 12288 | bytes 98304 | tf_op jit(solution)/shard_map/psum | solution.py:244
  1188.9 172.7 %all-reduce.3.cloned.1.call-done = bf16[512,96,128]{2,0,1:T(8,128)(2,1)} async-done(((bf16[512,96,128]{2,0,1:T(8,128)(2,1)}), bf16[512,96,128]{2,0,1:T(8,128)(2,1)}) %all-reduce.3.cloned.1.call-update) | async-done | bytes 12582928 | tf_op jit(solution)/shard_map/psum | solution.py:228
  1361.6 14.2 %reshape.255 = f32[512,96,128]{2,0,1:T(8,128)} convert(bf16[512,96,128]{2,0,1:T(8,128)(2,1)} %all-reduce.3.cloned.1.call-done) | non-fusion elementwise | flops 6291456 | bytes 37748736 | tf_op jit(solution)/shard_map/reshape | solution.py:229
  1375.8 8.9 gather_fusion.1
  1384.7 9.7 fusion.167
  (335 shorter events, 105.2 us)
Async XLA Ops:
  7.2 282.6 %all-gather.2.cloned.1.call-start = ((), (), s32[]{:S(2)}) async-start(), calls=%async_computation.1 | async-start | bytes 51904512 | tf_op jit(solution)/shard_map/all_gather | solution.py:104
  10.7 1083.9 %reduce-scatter.4.cloned.1.call-start = ((), (), s32[]{:S(2)}) async-start(), calls=%async_computation.3 | async-start | bytes 37748736
  11.4 6.5 copy-start.82
  11.4 7.8 copy-start.64
  18.1 289.1 %copy-start.79 = (s32[96]{0:T(128)}, s32[96]{0:T(128)S(1)}, u32[]{:S(2)}) copy-start(s32[96]{0:T(128)S(1)} %convert_reduce_fusion.6) | copy-start | bytes 1156
  380.7 18.1 %copy-start.30 = (bf16[1024,1024]{1,0:T(8,128)(2,1)S(1)}, bf16[1024,1024]{1,0:T(8,128)(2,1)}, u32[]{:S(2)}) copy-start(bf16[1024,1024]{1,0:T(8,128)(2,1)} %param.10) | copy-start | bytes 6291460
  398.8 12.3 copy-start.9
  413.6 54.5 %copy-start.10 = (bf16[1024,1024]{0,1:T(8,128)(2,1)}, bf16[1024,1024]{0,1:T(8,128)(2,1)S(1)}, u32[]{:S(2)}) copy-start(bf16[1024,1024]{0,1:T(8,128)(2,1)S(1)} %slice.372) | copy-start | bytes 6291460
  418.2 49.9 %copy-start.17 = (bf16[1024,1024]{0,1:T(8,128)(2,1)}, bf16[1024,1024]{0,1:T(8,128)(2,1)S(1)}, u32[]{:S(2)}) copy-start(bf16[1024,1024]{0,1:T(8,128)(2,1)S(1)} %get-tuple-element.93) | copy-start | bytes 6291460
  418.2 54.7 %copy-start.11 = (bf16[1024,1024]{0,1:T(8,128)(2,1)}, bf16[1024,1024]{0,1:T(8,128)(2,1)S(1)}, u32[]{:S(2)}) copy-start(bf16[1024,1024]{0,1:T(8,128)(2,1)S(1)} %get-tuple-element.92) | copy-start | bytes 6291460
  420.1 5.0 copy-start.3
  421.9 7.7 copy-start
  475.7 6.4 copy-start.33
  482.6 49.2 %copy-start.62 = (f32[1024]{0:T(1024)}, f32[1024]{0:T(1024)S(1)}, u32[]{:S(2)}) copy-start(f32[1024]{0:T(1024)S(1)} %multiply_reduce_fusion.11) | copy-start | bytes 12292
  483.4 48.4 %copy-start.77 = (f32[1,1024]{1,0:T(1,128)S(1)}, f32[1,1024]{1,0:T(1,128)}, u32[]{:S(2)}) copy-start(f32[1,1024]{1,0:T(1,128)} %get-tuple-element.100) | copy-start | bytes 12292
  531.7 14.4 %copy-start.8 = (bf16[1024,1024]{0,1:T(8,128)(2,1)S(1)}, bf16[1024,1024]{0,1:T(8,128)(2,1)}, u32[]{:S(2)}) copy-start(bf16[1024,1024]{0,1:T(8,128)(2,1)} %copy.68) | copy-start | bytes 6291460
  531.7 14.4 %copy-start.60 = (f32[1,1024]{1,0:T(1,128)S(1)}, f32[1,1024]{1,0:T(1,128)}, u32[]{:S(2)}) copy-start(f32[1,1024]{1,0:T(1,128)} %get-tuple-element.99) | copy-start | bytes 12292
  548.1 7.3 slice-start.32
  555.4 11.2 copy-start.38
  610.1 15.2 %copy-start.63 = (f32[1024]{0:T(1024)S(1)}, f32[1024]{0:T(1024)}, u32[]{:S(2)}) copy-start(f32[1024]{0:T(1024)} %copy-done.62) | copy-start | bytes 12292
  610.1 15.2 %copy-start.25 = (f32[1024,1024]{0,1:T(8,128)S(1)}, f32[1024,1024]{0,1:T(8,128)}, u32[]{:S(2)}) copy-start(f32[1024,1024]{0,1:T(8,128)} %get-tuple-element.131) | copy-start | bytes 12582916
  626.5 6.9 copy-start.70
  629.6 7.7 slice-start.12
  629.6 7.7 slice-start.13
  637.3 7.0 copy-start.21
  637.4 6.9 slice-start.16
  639.9 4.5 slice-start.17
  639.9 4.5 copy-start.54
  644.3 9.6 slice-start
  646.9 7.0 slice-start.1
  654.0 10.1 slice-start.18
  657.5 6.5 slice-start.19
  657.5 6.5 copy-start.55
  664.1 11.2 slice-start.8
  667.5 7.8 slice-start.9
  675.3 10.2 slice-start.20
  678.9 6.6 slice-start.21
  678.9 6.6 copy-start.56
  685.5 11.8 slice-start.4
  689.4 7.9 slice-start.5
  697.3 6.9 slice-start.24
  718.6 12.7 slice-start.22
  718.6 12.7 copy-start.26
  718.6 16.1 %slice-start.26 = ((s8[8388608]{0:T(1024)(128)(4,1)}), s8[4194304]{0:T(1024)(128)(4,1)S(1)}, s32[]{:S(2)}) async-start(s8[8388608]{0:T(1024)(128)(4,1)} %bitcast.325), calls=%async_computation.30 | async-start | bytes 8388608
  718.7 19.6 %slice-start.28 = ((s8[8388608]{0:T(1024)(128)(4,1)}), s8[4194304]{0:T(1024)(128)(4,1)S(1)}, s32[]{:S(2)}) async-start(s8[8388608]{0:T(1024)(128)(4,1)} %bitcast.329), calls=%async_computation.32 | async-start | bytes 8388608
  724.7 6.6 slice-start.23
  724.7 10.1 slice-start.27
  724.7 10.1 copy-start.27
  731.4 6.8 slice-start.14
  731.4 6.8 slice-start.29
  738.2 8.2 slice-start.2
  738.2 8.2 slice-start.3
  746.4 9.7 slice-start.10
  746.4 9.7 slice-start.30
  746.4 9.7 slice-start.11
  746.5 9.7 slice-start.31
  756.1 6.8 slice-start.6
  756.1 6.7 slice-start.7
  772.9 4.4 copy-start.31
  791.2 9.0 copy-start.23
  817.0 544.6 %all-reduce.3.cloned.1.call-start = ((), (), s32[]{:S(2)}) async-start(), calls=%async_computation.2 | async-start | bytes 25165824 | tf_op jit(solution)/shard_map/psum | solution.py:228
  1144.2 43.9 %copy-start.49 = (f32[12,1024]{1,0:T(8,128)S(1)}, f32[12,1024]{1,0:T(8,128)}, u32[]{:S(2)}) copy-start(f32[12,1024]{1,0:T(8,128)} %param.17) | copy-start | bytes 147460
  1144.3 43.9 %copy-start.58 = (f32[12,1024]{1,0:T(8,128)S(1)}, f32[12,1024]{1,0:T(8,128)}, u32[]{:S(2)}) copy-start(f32[12,1024]{1,0:T(8,128)} %param.18) | copy-start | bytes 147460
  1144.3 43.9 %copy-start.59 = (f32[12,1024]{1,0:T(8,128)S(1)}, f32[12,1024]{1,0:T(8,128)}, u32[]{:S(2)}) copy-start(f32[12,1024]{1,0:T(8,128)} %param.19) | copy-start | bytes 147460
  (56 other events, 141.2 us)
Sparse Core Ops, SparseCore 0:
  11.5 278.2 all-gather.1
  817.1 277.4 reduce-scatter.3
  1128.0 233.5 all-reduce.2
where the time goes:
time: 1410 us; the launch traced here: 1400 us
  waiting for transfers between devices  720 us (51%)
  matrix products  322 us (23%)
  local copies, waits for them, and re-layouts  178 us (13%)
  other arithmetic  123 us (9%)
  blocking collectives  41.2 us (3%)
  between operations  15.8 us (1%)
    unnamed x4, waiting for transfers between devices  278 us
    all_gather x1, waiting for transfers between devices, on_device(): gathered = lax.all_gather(halves, ('shard', 'replica'), axis=0, tiled=True)  270 us
    psum x1, waiting for transfers between devices, on_device(): summed = lax.psum(grad_shard, 'replica').astype(jnp.float32)  173 us
    select_n x1, local copies, waits for them, and re-layouts, on_device(): picked = jnp.take(grouped, slot_place, axis=1)  60.9 us
    dot_general x1, matrix products, on_device(): jnp.dot(normed_low, w_up, preferred_element_type=jnp.float32) + up_bias  48.3 us
    unnamed x241, local copies, waits for them, and re-layouts  41.5 us
    psum x1, blocking collectives, on_device(): lax.psum(jnp.concatenate([vector_terms, up_terms], axis=0), ('shard', 're...  41.2 us
    dot_general x8, matrix products, attend_back(): jnp.einsum('qhd,khd->hqk', grad_context, value_part, preferred_element_ty...  34.4 us
  transfers between devices with their start and end apart: 3, of which 3 were waited for; matrix products, arithmetic and copies ran while one was open for 2% of the time, Pallas kernels for 0%

commit v1 on v0

v1 whole, which is shorter than its diff:
```python
import functools
import math

import jax
import jax.numpy as jnp
from jax import lax
from jax.experimental import pallas as pl
from jax.experimental.pallas import tpu as pltpu
from jax.sharding import PartitionSpec as P

D = 1024
HEADS = 16
HEAD_DIM = 64
FF = 4096
STEP = 10
PAIR = 2 * HEAD_DIM
BOTH = ("shard", "replica")
VMEM_BYTES = 56 * 1024 * 1024
TILE = 1024
LANES = 128
BLOCKS = D // LANES

beta_one = 0.9
beta_two = 0.999
epsilon = 1e-08
rate_matrix = 0.05
rate_vector = 0.3
decay_rate = 0.01

NT = (((1,), (1,)), ((), ()))
TN = (((0,), (0,)), ((), ()))
EXPONENT = HEAD_DIM ** (-0.5) * math.log2(math.e)


def layer_norm(hidden, gain, shift):
    centered = hidden - jnp.mean(hidden, axis=-1, keepdims=True)
    spread = jnp.mean(centered * centered, axis=-1, keepdims=True)
    return centered * lax.rsqrt(spread + 1e-05) * gain + shift


def adamw(param, first, second, grad, rate, decay):
    first = beta_one * first + (1.0 - beta_one) * grad
    second = beta_two * second + (1.0 - beta_two) * grad * grad
    corrected = (
        first / (1.0 - beta_one**STEP) / (jnp.sqrt(second / (1.0 - beta_two**STEP)) + epsilon)
    )
    return (param - rate * (corrected + decay * param), first, second)


def head_masks():
    lane = lax.broadcasted_iota(jnp.int32, (1, PAIR), 1)
    first = (lane < HEAD_DIM).astype(jnp.float32)
    return (first.astype(jnp.bfloat16), (1.0 - first).astype(jnp.bfloat16))


def make_bias(seg_col_ref, seg_row_ref, bias_ref):
    @pl.when(pl.program_id(0) == 0)
    def _():
        same = seg_col_ref[...] == seg_row_ref[...]
        bias_ref[...] = jnp.where(same, 0.0, -1e30)


def attend_kernel(query_ref, key_ref, value_ref, seg_col_ref, seg_row_ref, context_ref, log_ref, bias_ref):
    make_bias(seg_col_ref, seg_row_ref, bias_ref)
    masks = head_masks()
    keys = key_ref[...]
    values = value_ref[...]
    length = keys.shape[0]
    block = 512
    lane = lax.broadcasted_iota(jnp.int32, (block, PAIR), 1)
    for first_row in range(0, length, block):
        rows = pl.ds(first_row, block)
        query = query_ref[rows, :]
        total = jnp.zeros((block, PAIR), jnp.float32)
        logs = jnp.zeros((block, PAIR), jnp.float32)
        for head, mask in enumerate(masks):
            scores = lax.dot_general(query * mask, keys, NT, preferred_element_type=jnp.float32)
            scores = scores + bias_ref[rows, :]
            top = jnp.max(scores, axis=1, keepdims=True)
            expd = jnp.exp2((scores - top) * EXPONENT)
            norm = jnp.sum(expd, axis=1, keepdims=True)
            part = jnp.dot(expd.astype(jnp.bfloat16), values * mask, preferred_element_type=jnp.float32)
            total = total + part * (1.0 / norm)
            logs = jnp.where(lane == head, top * EXPONENT + jnp.log2(norm), logs)
        context_ref[rows, :] = total.astype(jnp.bfloat16)
        log_ref[0, :, rows] = jnp.transpose(logs)[:8, :]


def kernel_call(kernel, name, grid, in_specs, operands, out_specs, out_shape, scratch, flops, places=None, after=(), aliases=None):
    count, prefetch = len(after), 0 if places is None else 1

    def body(*refs):
        kernel(*refs[:prefetch], *refs[prefetch + count :])

    moved = sum(math.prod(array.shape) * array.dtype.itemsize for array in operands)
    made = jax.tree.leaves(out_shape)
    moved += sum(math.prod(array.shape) * array.dtype.itemsize for array in made)
    return pl.pallas_call(
        body,
        grid_spec=pltpu.PrefetchScalarGridSpec(
            num_scalar_prefetch=prefetch,
            grid=grid,
            in_specs=[pl.BlockSpec(memory_space=pl.ANY)] * count + list(in_specs),
            out_specs=out_specs,
            scratch_shapes=scratch,
        ),
        out_shape=out_shape,
        input_output_aliases={prefetch + count + k: v for k, v in (aliases or {}).items()},
        compiler_params=pltpu.CompilerParams(vmem_limit_bytes=VMEM_BYTES),
        cost_estimate=pl.CostEstimate(flops=flops // 16, bytes_accessed=moved // 16, transcendentals=0),
        name=name,
    )(*([] if places is None else [places]), *after, *operands)


def attend(projected, seg_col, seg_row, first_pair, pair_count, earlier, after=()):
    length = projected.shape[0]
    pairs = D // PAIR

    def spec(offset):
        return pl.BlockSpec((length, PAIR), lambda i: (0, offset + first_pair + i))

    in_specs = [
        spec(0),
        spec(pairs),
        spec(2 * pairs),
        pl.BlockSpec((length, 1), lambda i: (0, 0)),
        pl.BlockSpec((1, length), lambda i: (0, 0)),
    ]
    operands = [projected, projected, projected, seg_col, seg_row]
    kernel, aliases = attend_kernel, None
    if earlier is not None:
        in_specs += [pl.BlockSpec(memory_space=pl.ANY)] * 2
        operands += list(earlier)
        aliases = {5: 0, 6: 1}
        kernel = lambda *refs: attend_kernel(*refs[:5], *refs[7:])
    return kernel_call(
        kernel,
        "attend",
        (pair_count,),
        in_specs,
        operands,
        [spec(0), pl.BlockSpec((1, 8, length), lambda i: (first_pair + i, 0, 0))],
        [
            jax.ShapeDtypeStruct((length, D), jnp.bfloat16),
            jax.ShapeDtypeStruct((pairs, 8, length), jnp.float32),
        ],
        [pltpu.VMEM((length, length), jnp.float32)],
        16 * 2 * pair_count * length * length * HEAD_DIM,
        after=after,
        aliases=aliases,
    )


def attend_back_kernel(
    query_ref, key_ref, value_ref, context_ref, grad_ref, log_ref, seg_col_ref, seg_row_ref,
    grad_ref_all, sum_ref, bias_ref,
):
    make_bias(seg_col_ref, seg_row_ref, bias_ref)
    masks = head_masks()
    query = query_ref[...]
    grad = grad_ref[...]
    length = query.shape[0]
    block = 1024
    row_id = lax.broadcasted_iota(jnp.int32, (8, PAIR), 0)
    lane_id = lax.broadcasted_iota(jnp.int32, (8, PAIR), 1)
    chooser = (lane_id // HEAD_DIM == row_id).astype(jnp.float32)
    product = grad.astype(jnp.float32) * context_ref[...].astype(jnp.float32)
    inner = lax.dot_general(
        chooser, product, NT, precision=lax.Precision.HIGHEST, preferred_element_type=jnp.float32
    )
    grad_query = jnp.zeros((PAIR, length), jnp.float32)
    value_sum = jnp.zeros((1, PAIR), jnp.float32)
    for first_row in range(0, length, block):
        rows = pl.ds(first_row, block)
        keys = key_ref[rows, :]
        values = value_ref[rows, :]
        grad_key = jnp.zeros((block, PAIR), jnp.float32)
        grad_value = jnp.zeros((block, PAIR), jnp.float32)
        for head, mask in enumerate(masks):
            key_head = keys * mask
            scores = lax.dot_general(key_head, query, NT, preferred_element_type=jnp.float32)
            scores = scores + bias_ref[rows, :]
            probs = jnp.exp2(scores * EXPONENT - log_ref[0, head : head + 1, :])
            grad_probs = lax.dot_general(values * mask, grad, NT, preferred_element_type=jnp.float32)
            grad_scores = (probs * (grad_probs - inner[head : head + 1, :])).astype(jnp.bfloat16)
            grad_value = grad_value + jnp.dot(
                probs.astype(jnp.bfloat16), grad * mask, preferred_element_type=jnp.float32
            )
            grad_key = grad_key + jnp.dot(
                grad_scores, query * mask, preferred_element_type=jnp.float32
            )
            grad_query = grad_query + lax.dot_general(
                key_head, grad_scores, TN, preferred_element_type=jnp.float32
            )
        grad_ref_all[1, rows, :] = (grad_key * HEAD_DIM ** (-0.5)).astype(jnp.bfloat16)
        grad_value = grad_value.astype(jnp.bfloat16)
        grad_ref_all[2, rows, :] = grad_value
        value_sum = value_sum + jnp.sum(grad_value.astype(jnp.float32), axis=0, keepdims=True)
    grad_query = jnp.transpose(grad_query * HEAD_DIM ** (-0.5)).astype(jnp.bfloat16)
    grad_ref_all[0] = grad_query
    query_sum = jnp.sum(grad_query.astype(jnp.float32), axis=0, keepdims=True)
    sum_ref[0] = jnp.where(row_id == 0, query_sum, value_sum)


def attend_back(
    projected, context, grad_context, logs, seg_col, seg_row, first_pair, pair_count, half_first, half_count, earlier, after=()
):
    length = projected.shape[0]
    pairs = D // PAIR
    shift = first_pair - half_first

    def spec(offset):
        return pl.BlockSpec((length, PAIR), lambda i: (0, offset + first_pair + i))

    in_specs = [
        spec(0),
        spec(pairs),
        spec(2 * pairs),
        spec(0),
        spec(0),
        pl.BlockSpec((1, 8, length), lambda i: (first_pair + i, 0, 0)),
        pl.BlockSpec((length, 1), lambda i: (0, 0)),
        pl.BlockSpec((1, length), lambda i: (0, 0)),
    ]
    operands = [projected, projected, projected, context, grad_context, logs, seg_col, seg_row]
    kernel, aliases = attend_back_kernel, None
    if earlier is not None:
        in_specs += [pl.BlockSpec(memory_space=pl.ANY)] * 2
        operands += list(earlier)
        aliases = {8: 0, 9: 1}
        kernel = lambda *refs: attend_back_kernel(*refs[:8], *refs[10:])
    return kernel_call(
        kernel,
        "attend_back",
        (pair_count,),
        in_specs,
        operands,
        [
            pl.BlockSpec((3, length, PAIR), lambda i: (0, 0, shift + i)),
            pl.BlockSpec((1, 8, PAIR), lambda i: (shift + i, 0, 0)),
        ],
        [
            jax.ShapeDtypeStruct((3, length, half_count * PAIR), jnp.bfloat16),
            jax.ShapeDtypeStruct((half_count, 8, PAIR), jnp.float32),
        ],
        [pltpu.VMEM((length, length), jnp.float32)],
        40 * 2 * pair_count * length * length * HEAD_DIM,
        after=after,
        aliases=aliases,
    )


def joined(piece_refs):
    if len(piece_refs) == 1:
        return piece_refs[0][...]
    return jnp.concatenate([ref[...] for ref in piece_refs], axis=0)


def block_at(place_ref, index):
    return pl.ds(pl.multiple_of(place_ref[index] * LANES, LANES), LANES)


def to_pieces(place_ref, from_ref, to_ref):
    for index in range(BLOCKS):
        to_ref[:, index * LANES : (index + 1) * LANES] = from_ref[:, block_at(place_ref, index)]


def from_pieces(place_ref, from_ref, to_ref):
    for index in range(BLOCKS):
        part = from_ref[:, index * LANES : (index + 1) * LANES]
        to_ref[:, block_at(place_ref, index)] = part.astype(to_ref.dtype)


def tile_specs(pieces, tile_of):
    return [pl.BlockSpec((piece.shape[0], TILE), lambda j, *_: (0, tile_of(j))) for piece in pieces]


def whole(*shape):
    return pl.BlockSpec(shape, lambda j, *_: (0,) * len(shape))


ANYWHERE = pl.BlockSpec(memory_space=pl.ANY)


def whole_once(*shape):
    return pl.BlockSpec(shape, lambda j, *_: (0,) * len(shape), pipeline_mode=pl.Buffered(1))


def project_kernel(place_ref, input_ref, bias_ref, *refs):
    pieces, (out_ref, turned_ref) = refs[:-2], refs[-2:]

    @pl.when(pl.program_id(0) == 0)
    def _():
        to_pieces(place_ref, input_ref, turned_ref)

    weights, bias = joined(pieces), bias_ref[...]
    block = 512
    for first_row in range(0, turned_ref.shape[0], block):
        rows = pl.ds(first_row, block)
        made = jnp.dot(turned_ref[rows, :], weights, preferred_element_type=jnp.float32)
        out_ref[rows, :] = (made + bias).astype(jnp.bfloat16)


def project(inputs, bias, weight, places, after=()):
    rows = inputs.shape[0]
    columns = weight[0].shape[1]
    return kernel_call(
        project_kernel,
        "project",
        (columns // TILE,),
        [whole_once(rows, D), pl.BlockSpec((1, TILE), lambda j, *_: (0, j))] + tile_specs(weight, lambda j: j),
        [inputs, bias, *weight],
        pl.BlockSpec((rows, TILE), lambda j, *_: (0, j)),
        jax.ShapeDtypeStruct((rows, columns), jnp.bfloat16),
        [pltpu.VMEM((rows, D), jnp.bfloat16)],
        2 * rows * D * columns,
        places=places,
        after=after,
    )


def row_loop(rows_all, block, body, start):
    def step(index, carry):
        return body(pl.ds(pl.multiple_of(index * block, block), block), carry)

    return lax.fori_loop(0, rows_all // block, step, start)


def gelu_tile(turned_ref, weights, bias, active_ref, slope_ref):
    block = 512
    for first_row in range(0, turned_ref.shape[0], block):
        rows = pl.ds(first_row, block)
        upward = jnp.dot(turned_ref[rows, :], weights, preferred_element_type=jnp.float32) + bias
        cumulative = 0.5 + 0.5 * lax.erf(upward * (2.0**-0.5))
        density = jnp.exp2(upward * upward * (-0.5 * math.log2(math.e))) * (2.0 * math.pi) ** -0.5
        active_ref[rows, :] = (upward * cumulative).astype(jnp.bfloat16)
        slope_ref[rows, :] = (cumulative + upward * density).astype(jnp.bfloat16)


def out_up_kernel(place_ref, vector_ref, bias_ref, context_ref, token_ref, *refs):
    pieces = refs[:-10]
    unit_out, spread_ref, low_out, active_ref, slope_ref, turned_ref, attn_ref, unit_ref, low_ref, sems = refs[-10:]
    step = pl.program_id(0)
    rows_all = context_ref.shape[0]

    def leaving():
        return [
            pltpu.make_async_copy(unit_ref, unit_out, sems.at[0]),
            pltpu.make_async_copy(low_ref, low_out, sems.at[1]),
        ]

    @pl.when(step == 0)
    def _():
        to_pieces(place_ref, context_ref, turned_ref)
        attn_ref[...] = jnp.dot(turned_ref[...], joined(pieces), preferred_element_type=jnp.float32)

        def normalise(rows, carry):
            hidden = token_ref[rows, :].astype(jnp.float32) + (attn_ref[rows, :] + vector_ref[2:3, :])
            centered = hidden - jnp.mean(hidden, axis=1, keepdims=True)
            spread = lax.rsqrt(jnp.mean(centered * centered, axis=1, keepdims=True) + 1e-05)
            unit = centered * spread
            unit_ref[rows, :] = unit
            spread_ref[rows, :] = jnp.broadcast_to(spread, (unit.shape[0], LANES))
            low_ref[rows, :] = (unit * vector_ref[3:4, :] + vector_ref[4:5, :]).astype(jnp.bfloat16)
            return carry

        row_loop(rows_all, 128, normalise, 0)
        for copy in leaving():
            copy.start()
        to_pieces(place_ref, low_ref, turned_ref)

    @pl.when(step > 0)
    def _():
        gelu_tile(turned_ref, joined(pieces), bias_ref[...], active_ref, slope_ref)

    @pl.when(step == pl.num_programs(0) - 1)
    def _():
        for copy in leaving():
            copy.wait()


def out_up(context, tokens, vectors, up_bias, weight, places, up_tiles, after=()):
    rows = context.shape[0]
    late = lambda j, *_: (0, jnp.maximum(j - 1, 0))
    return kernel_call(
        out_up_kernel,
        "out_up",
        (1 + up_tiles,),
        [whole_once(*vectors.shape), pl.BlockSpec((1, TILE), late), whole_once(rows, D), whole_once(rows, D)]
        + tile_specs(weight, lambda j: j),
        [vectors, up_bias, context, tokens, *weight],
        [
            ANYWHERE,
            whole(rows, LANES),
            ANYWHERE,
            pl.BlockSpec((rows, TILE), late),
            pl.BlockSpec((rows, TILE), late),
        ],
        [
            jax.ShapeDtypeStruct((rows, D), jnp.float32),
            jax.ShapeDtypeStruct((rows, LANES), jnp.float32),
            jax.ShapeDtypeStruct((rows, D), jnp.bfloat16),
            jax.ShapeDtypeStruct((rows, FF), jnp.bfloat16),
            jax.ShapeDtypeStruct((rows, FF), jnp.bfloat16),
        ],
        [
            pltpu.VMEM((rows, D), jnp.bfloat16),
            pltpu.VMEM((rows, D), jnp.float32),
            pltpu.VMEM((rows, D), jnp.float32),
            pltpu.VMEM((rows, D), jnp.bfloat16),
            pltpu.SemaphoreType.DMA((2,)),
        ],
        2 * rows * D * (1 + up_tiles) * TILE,
        places=places,
        after=after,
    )


def up_rest_kernel(place_ref, bias_ref, low_ref, *refs):
    pieces, (active_ref, slope_ref, turned_ref) = refs[:-5], refs[-3:]

    @pl.when(pl.program_id(0) == 0)
    def _():
        to_pieces(place_ref, low_ref, turned_ref)

    gelu_tile(turned_ref, joined(pieces), bias_ref[...], active_ref, slope_ref)


def up_rest(normed_low, up_bias, weight, places, first_tile, filled, after=()):
    rows = normed_low.shape[0]
    at = lambda j, *_: (0, first_tile + j)
    tiles = FF // TILE - first_tile
    count = len(weight)
    return kernel_call(
        up_rest_kernel,
        "up_rest",
        (tiles,),
        [pl.BlockSpec((1, TILE), at), whole_once(rows, D)]
        + tile_specs(weight, lambda j: 1 + first_tile + j)
        + [pl.BlockSpec(memory_space=pl.ANY)] * 2,
        [up_bias, normed_low, *weight, *filled],
        [pl.BlockSpec((rows, TILE), at)] * 2,
        [jax.ShapeDtypeStruct((rows, FF), jnp.bfloat16)] * 2,
        [pltpu.VMEM((rows, D), jnp.bfloat16)],
        2 * rows * D * tiles * TILE,
        places=places,
        after=after,
        aliases={2 + count: 0, 3 + count: 1},
    )


def column_sum(values):
    return jnp.sum(values, axis=0, keepdims=True)


def down_kernel(place_ref, vector_ref, unit_in, cotangent_in, active_ref, slope_ref, *refs):
    pieces, (out_out, second_out, branch_out, grad_up_ref, sum_ref, up_sum_ref) = refs[:-14], refs[-14:-8]
    total_ref, turned_ref, unit_ref, cotangent_ref, out_ref, second_ref, branch_ref, sems = refs[-8:]
    step = pl.program_id(0)
    rows_all = active_ref.shape[0]
    tiles = FF // TILE

    def coming():
        return [
            pltpu.make_async_copy(unit_in, unit_ref, sems.at[0]),
            pltpu.make_async_copy(cotangent_in, cotangent_ref, sems.at[1]),
        ]

    def leaving():
        return [
            pltpu.make_async_copy(out_ref, out_out, sems.at[2]),
            pltpu.make_async_copy(second_ref, second_out, sems.at[3]),
            pltpu.make_async_copy(branch_ref, branch_out, sems.at[4]),
        ]

    @pl.when(step == 0)
    def _():
        for copy in coming():
            copy.start()
        total_ref[...] = lax.dot_general(
            active_ref[...], joined(pieces), NT, preferred_element_type=jnp.float32
        )

    @pl.when((step > 0) & (step < tiles))
    def _():
        total_ref[...] += lax.dot_general(
            active_ref[...], joined(pieces), NT, preferred_element_type=jnp.float32
        )

    @pl.when(step == tiles)
    def _():
        from_pieces(place_ref, total_ref, second_ref)
        for copy in coming():
            copy.wait()

        def normalise(rows, carry):
            normed = unit_ref[rows, :] * vector_ref[3:4, :] + vector_ref[4:5, :]
            hidden = normed + (second_ref[rows, :] + vector_ref[5:6, :])
            centered = hidden - jnp.mean(hidden, axis=1, keepdims=True)
            spread = lax.rsqrt(jnp.mean(centered * centered, axis=1, keepdims=True) + 1e-05)
            unit = centered * spread
            out_ref[rows, :] = (unit * vector_ref[6:7, :] + vector_ref[7:8, :]).astype(jnp.bfloat16)
            grad = cotangent_ref[rows, :].astype(jnp.float32)
            scaled = grad * vector_ref[6:7, :]
            mean_one = jnp.mean(scaled, axis=1, keepdims=True)
            mean_two = jnp.mean(scaled * unit, axis=1, keepdims=True)
            second = spread * (scaled - mean_one - unit * mean_two)
            second_ref[rows, :] = second
            branch = second.astype(jnp.bfloat16)
            branch_ref[rows, :] = branch
            return (
                carry[0] + column_sum(branch.astype(jnp.float32)),
                carry[1] + column_sum(grad * unit),
                carry[2] + column_sum(grad),
            )

        zero = jnp.zeros((1, D), jnp.float32)
        sums = row_loop(rows_all, 128, normalise, (zero, zero, zero))
        for index, value in enumerate(sums):
            sum_ref[index : index + 1, :] = value
        for copy in leaving():
            copy.start()
        to_pieces(place_ref, branch_ref, turned_ref)

    @pl.when(step >= tiles)
    def _():
        grad = jnp.dot(turned_ref[...], joined(pieces), preferred_element_type=jnp.float32)
        grad = (grad * slope_ref[...].astype(jnp.float32)).astype(jnp.bfloat16)
        grad_up_ref[...] = grad
        up_sum_ref[...] = column_sum(grad.astype(jnp.float32))

    @pl.when(step == 2 * tiles - 1)
    def _():
        for copy in leaving():
            copy.wait()


def down_both(unit, cotangent, active, slope, vectors, weight, places, after=()):
    rows = unit.shape[0]
    tiles = FF // TILE
    early = lambda j, *_: (0, jnp.minimum(j, tiles - 1))
    late = lambda j, *_: (0, jnp.maximum(j - tiles, 0))
    return kernel_call(
        down_kernel,
        "down_both",
        (2 * tiles,),
        [
            whole_once(*vectors.shape),
            ANYWHERE,
            ANYWHERE,
            pl.BlockSpec((rows, TILE), early),
            pl.BlockSpec((rows, TILE), late),
        ]
        + tile_specs(weight, lambda j: j % tiles),
        [vectors, unit, cotangent, active, slope, *weight],
        [
            ANYWHERE,
            ANYWHERE,
            ANYWHERE,
            pl.BlockSpec((rows, TILE), late),
            whole(8, D),
            pl.BlockSpec((1, TILE), late),
        ],
        [
            jax.ShapeDtypeStruct((rows, D), jnp.bfloat16),
            jax.ShapeDtypeStruct((rows, D), jnp.float32),
            jax.ShapeDtypeStruct((rows, D), jnp.bfloat16),
            jax.ShapeDtypeStruct((rows, FF), jnp.bfloat16),
            jax.ShapeDtypeStruct((8, D), jnp.float32),
            jax.ShapeDtypeStruct((1, FF), jnp.float32),
        ],
        [
            pltpu.VMEM((rows, D), jnp.float32),
            pltpu.VMEM((rows, D), jnp.bfloat16),
            pltpu.VMEM((rows, D), jnp.float32),
            pltpu.VMEM((rows, D), jnp.bfloat16),
            pltpu.VMEM((rows, D), jnp.bfloat16),
            pltpu.VMEM((rows, D), jnp.float32),
            pltpu.VMEM((rows, D), jnp.bfloat16),
            pltpu.SemaphoreType.DMA((5,)),
        ],
        4 * rows * D * FF,
        places=places,
        after=after,
    )


def up_back_kernel(place_ref, vector_ref, unit_in, spread_ref, second_in, grad_up_ref, *refs):
    pieces, (first_out, attn_out, context_ref, sum_ref) = refs[:-10], refs[-10:-6]
    total_ref, unit_ref, second_ref, first_ref, attn_ref, sems = refs[-6:]
    step = pl.program_id(0)
    rows_all = unit_ref.shape[0]
    tiles = FF // TILE
    out_tiles = D // TILE

    def product(left):
        return lax.dot_general(left, joined(pieces), NT, preferred_element_type=jnp.float32)

    def coming():
        return [
            pltpu.make_async_copy(unit_in, unit_ref, sems.at[0]),
            pltpu.make_async_copy(second_in, second_ref, sems.at[1]),
        ]

    def leaving():
        return [
            pltpu.make_async_copy(first_ref, first_out, sems.at[2]),
            pltpu.make_async_copy(attn_ref, attn_out, sems.at[3]),
        ]

    @pl.when(step == 0)
    def _():
        for copy in coming():
            copy.start()
        total_ref[...] = product(grad_up_ref[...])

    @pl.when((step > 0) & (step < tiles))
    def _():
        total_ref[...] += product(grad_up_ref[...])

    @pl.when(step == tiles)
    def _():
        from_pieces(place_ref, total_ref, first_ref)
        for copy in coming():
            copy.wait()

        def normalise(rows, carry):
            grad = second_ref[rows, :] + first_ref[rows, :]
            unit = unit_ref[rows, :]
            scaled = grad * vector_ref[3:4, :]
            mean_one = jnp.mean(scaled, axis=1, keepdims=True)
            mean_two = jnp.mean(scaled * unit, axis=1, keepdims=True)
            first = spread_ref[rows, :1] * (scaled - mean_one - unit * mean_two)
            first_ref[rows, :] = first
            attn = first.astype(jnp.bfloat16)
            attn_ref[rows, :] = attn
            return (
                carry[0] + column_sum(attn.astype(jnp.float32)),
                carry[1] + column_sum(grad * unit),
                carry[2] + column_sum(grad),
            )

        zero = jnp.zeros((1, D), jnp.float32)
        sums = row_loop(rows_all, 128, normalise, (zero, zero, zero))
        for index, value in enumerate(sums):
            sum_ref[index : index + 1, :] = value
        for copy in leaving():
            copy.start()

    for tile in range(out_tiles):

        @pl.when(step == tiles + tile)
        def _():
            made = product(attn_ref[:, tile * TILE : (tile + 1) * TILE])
            total_ref[...] = made if tile == 0 else total_ref[...] + made

    @pl.when(step == tiles + out_tiles - 1)
    def _():
        from_pieces(place_ref, total_ref, context_ref)
        for copy in leaving():
            copy.wait()


def up_back(unit, spread, second, grad_up, vectors, weight, places, after=()):
    rows = unit.shape[0]
    tiles = FF // TILE
    out_tiles = D // TILE
    return kernel_call(
        up_back_kernel,
        "up_back",
        (tiles + out_tiles,),
        [
            whole_once(*vectors.shape),
            ANYWHERE,
            whole_once(rows, LANES),
            ANYWHERE,
            pl.BlockSpec((rows, TILE), lambda j, *_: (0, jnp.minimum(j, tiles - 1))),
        ]
        + tile_specs(weight, lambda j: (j + out_tiles) % (tiles + out_tiles)),
        [vectors, unit, spread, second, grad_up, *weight],
        [ANYWHERE, ANYWHERE, whole(rows, D), whole(8, D)],
        [
            jax.ShapeDtypeStruct((rows, D), jnp.float32),
            jax.ShapeDtypeStruct((rows, D), jnp.bfloat16),
            jax.ShapeDtypeStruct((rows, D), jnp.bfloat16),
            jax.ShapeDtypeStruct((8, D), jnp.float32),
        ],
        [
            pltpu.VMEM((rows, D), jnp.float32),
            pltpu.VMEM((rows, D), jnp.float32),
            pltpu.VMEM((rows, D), jnp.float32),
            pltpu.VMEM((rows, D), jnp.float32),
            pltpu.VMEM((rows, D), jnp.bfloat16),
            pltpu.SemaphoreType.DMA((4,)),
        ],
        2 * rows * D * (D + FF),
        places=places,
        after=after,
    )


def input_back_kernel(place_ref, first_in, one_ref, two_ref, *refs):
    pieces, (out_ref, total_ref, first_ref, sem) = refs[:-4], refs[-4:]
    step = pl.program_id(0)
    coming = pltpu.make_async_copy(first_in, first_ref, sem)

    def product():
        grad = jnp.concatenate([one_ref[0], two_ref[0]], axis=1)
        return lax.dot_general(grad, joined(pieces), NT, preferred_element_type=jnp.float32)

    @pl.when(step == 0)
    def _():
        coming.start()
        total_ref[...] = product()

    @pl.when(step > 0)
    def _():
        total_ref[...] += product()

    @pl.when(step == 2)
    def _():
        coming.wait()
        for index in range(BLOCKS):
            columns = block_at(place_ref, index)
            part = first_ref[:, columns] + total_ref[:, index * LANES : (index + 1) * LANES]
            out_ref[:, columns] = part.astype(jnp.bfloat16)


def input_back(first, grad_one, grad_two, weight, places, after=()):
    rows = first.shape[0]
    half = pl.BlockSpec((1, rows, D // 2), lambda j, *_: (j, 0, 0))
    return kernel_call(
        input_back_kernel,
        "input_back",
        (3,),
        [ANYWHERE, half, half] + tile_specs(weight, lambda j: j),
        [first, grad_one, grad_two, *weight],
        whole(rows, D),
        jax.ShapeDtypeStruct((rows, D), jnp.bfloat16),
        [pltpu.VMEM((rows, D), jnp.float32), pltpu.VMEM((rows, D), jnp.float32), pltpu.SemaphoreType.DMA],
        2 * rows * D * 3 * D,
        places=places,
        after=after,
    )


def weight_grad_kernel(place_ref, *refs, spans):
    count = len(spans)
    left_refs, right_refs = refs[:count], refs[count : 2 * count]
    out_refs, turned_ref = refs[2 * count : -1], refs[-1]
    step = pl.program_id(0)
    for index, (first, last) in enumerate(spans):

        @pl.when(step == first)
        def _():
            for place in range(BLOCKS):
                turned_ref[pl.ds(place * LANES, LANES), :] = jnp.transpose(
                    left_refs[index][:, block_at(place_ref, place)]
                )

        @pl.when((step >= first) & (step < last))
        def _():
            grad = jnp.dot(turned_ref[...], right_refs[index][0], preferred_element_type=jnp.float32)
            grad = grad.astype(jnp.bfloat16)
            first_row = 0
            for out_ref in out_refs:
                out_ref[...] = grad[first_row : first_row + out_ref.shape[0]]
                first_row += out_ref.shape[0]


def weight_grad(pairs, places, after=()):
    rows = pairs[0][0].shape[0]
    tile_width = min(TILE, *[right.shape[2] for _, right in pairs])
    in_specs, right_specs, operands, rights, spans = [], [], [], [], []
    step = 0
    for left, right in pairs:
        groups, _, width = right.shape
        per_group = width // tile_width
        first, last = step, step + groups * per_group
        step = last
        spans.append((first, last))
        in_specs.append(whole_once(rows, D))
        operands.append(left)

        def right_at(j, place, first=first, last=last, per_group=per_group):
            tile = jnp.clip(j - first, 0, last - first - 1)
            return (tile // per_group, 0, tile % per_group)

        right_specs.append(pl.BlockSpec((1, rows, tile_width), right_at))
        rights.append(right)
    columns = step * tile_width
    heights = [LANES] * 3 + [LANES // 2] * 2 + [4 * LANES]
    return kernel_call(
        functools.partial(weight_grad_kernel, spans=spans),
        "weight_grad",
        (step,),
        in_specs + right_specs,
        operands + rights,
        [pl.BlockSpec((height, tile_width), lambda j, place: (0, j)) for height in heights],
        [jax.ShapeDtypeStruct((height, columns), jnp.bfloat16) for height in heights],
        [pltpu.VMEM((D, rows), jnp.bfloat16)],
        2 * D * rows * columns,
        places=places,
        after=after,
    )


def gate(value, *others):
    return lax.optimization_barrier((value, *others))[0]


def picked(array, places):
    return array.at[places].get(mode="promise_in_bounds")


def wide(value):
    return value.astype(jnp.float32)


class WholeMesh:
    def __init__(self, shard_count, replica_count):
        self.replica_count = replica_count
        self.places = jnp.arange(BLOCKS, dtype=jnp.int32)

    def split_rows(self, slots, slab):
        count, _, width = slots.shape
        return slots.reshape(count, self.replica_count, slab, width).transpose(1, 0, 2, 3)

    def join_rows(self, slabs):
        replicas, count, slab, width = slabs.shape
        return slabs.transpose(1, 0, 2, 3).reshape(count, replicas * slab, width)

    def spread(self, slots, owners, slot_of, slab):
        sent = self.split_rows(slots, slab)
        heard = lax.all_to_all(sent, "replica", split_axis=0, concat_axis=0, tiled=True)
        return picked(heard.reshape(-1, *heard.shape[2:]), owners * slots.shape[0] + slot_of)

    def collect(self, stripes, stripe_at, heavy):
        sent = picked(stripes, stripe_at)
        return self.join_rows(lax.all_to_all(sent, "replica", split_axis=0, concat_axis=0, tiled=True))

    def gather_line(self, mine):
        return lax.all_gather(mine, BOTH, axis=0, tiled=True)

    def gather_near(self, block):
        return [block]

    def gather_far(self, pieces):
        return []

    def gather_core(self, pieces):
        return []

    def scatter_core(self, pairs, after=()):
        parts = [
            lax.dot_general(left, group, TN, preferred_element_type=jnp.float32)
            for left, right in pairs
            for group in right
        ]
        part = jnp.concatenate(parts, axis=1).astype(jnp.bfloat16)
        return [lax.psum_scatter(part, BOTH, scatter_dimension=0, tiled=True)]

    def scatter_near(self, parts):
        return parts

    def scatter_far(self, parts):
        return parts

    def scatter_half(self, parts):
        return parts

    def scatter_slab(self, parts):
        return parts

    def scatter_line(self, parts):
        return parts

    def scatter_end(self, parts):
        return parts[0]

    def total_step(self, part, kind):
        return jnp.sum(lax.all_gather(part, BOTH, axis=0), axis=0) if kind == "core" else part


class BlockMesh:
    def __init__(self, shard_count, replica_count):
        index = lax.axis_index("replica")
        self.y = lax.axis_index("shard")
        self.z, self.x, self.core = index // 4, (index // 2) % 2, index % 2

        def places(core):
            return [
                (self.y ^ dy) * 4 + core * 2 + (self.x ^ dx) for dx, dy in ((0, 0), (1, 0), (0, 1), (1, 1))
            ]

        self.own = jnp.stack(places(self.core)).astype(jnp.int32)
        self.partner = jnp.stack(places(1 - self.core)).astype(jnp.int32)
        self.places = jnp.concatenate([self.own, self.partner])

    def swap(self, array, bits):
        return lax.ppermute(array, "replica", [(r, r ^ bits) for r in range(16)])

    def swap_core(self, array):
        return self.swap(array, 1)

    def swap_x(self, array):
        return self.swap(array, 2)

    def swap_y(self, array):
        return lax.ppermute(array, "shard", [(0, 1), (1, 0)])

    def swap_z(self, array, bits):
        return self.swap(array, 4 * bits)

    def split_rows(self, slots, slab):
        count, _, width = slots.shape
        parts = slots.reshape(count, 2, 2, 4, slab, width).transpose(3, 2, 1, 0, 4, 5)
        return parts.reshape(16, count, slab, width)

    def join_rows(self, slabs):
        _, count, slab, width = slabs.shape
        parts = slabs.reshape(4, 2, 2, count, slab, width).transpose(3, 2, 1, 0, 4, 5)
        return parts.reshape(count, 16 * slab, width)

    def spread(self, slots, owners, slot_of, slab):
        count = owners.shape[0] // 16
        sent = self.split_rows(slots[:count], slab)
        heard = lax.all_to_all(sent, "replica", split_axis=0, concat_axis=0, tiled=True)
        rest = self.split_rows(slots[count:], slab)
        rest = rest.reshape(4, 2, 2, *rest.shape[1:])
        heavy = jnp.max(jnp.where(slot_of >= count, owners, 0))
        odd = self.core == 1
        keep, send = jnp.where(odd, rest[:, :, 1], rest[:, :, 0]), jnp.where(odd, rest[:, :, 0], rest[:, :, 1])
        rest = jnp.where(heavy % 2 == self.core, keep, self.swap_core(send))
        odd = self.x == 1
        keep, send = jnp.where(odd, rest[:, 1], rest[:, 0]), jnp.where(odd, rest[:, 0], rest[:, 1])
        rest = jnp.where((heavy // 2) % 2 == self.x, keep, self.swap_x(send))
        away = (heavy // 4) ^ self.z
        last = lax.dynamic_index_in_dim(rest, self.z, 0, keepdims=False)
        for bits in (1, 2, 3):
            other = lax.dynamic_index_in_dim(rest, self.z ^ bits, 0, keepdims=False)
            last = jnp.where(away == bits, self.swap_z(other, bits), last)
        heard = jnp.concatenate([heard.reshape(-1, *heard.shape[2:]), last], axis=0)
        place = jnp.where(slot_of < count, owners * count + slot_of, 16 * count + slot_of - count)
        return picked(heard, place)

    def collect(self, stripes, stripe_at, heavy):
        count = stripes.shape[0] // 16
        sent = picked(stripes, stripe_at[:, :count])
        extra = lax.dynamic_index_in_dim(stripe_at, heavy, 0, keepdims=False)[count:]
        rest = picked(gate(stripes, sent), extra)
        heard = lax.all_to_all(sent, "replica", split_axis=0, concat_axis=0, tiled=True)
        rest = jnp.stack(self.in_order([rest] + [self.swap_z(rest, bits) for bits in (1, 2, 3)]))
        other = self.swap_x(rest)
        odd = self.x == 1
        rest = jnp.stack([jnp.where(odd, other, rest), jnp.where(odd, rest, other)], axis=1)
        other = self.swap_core(rest)
        odd = self.core == 1
        rest = jnp.stack([jnp.where(odd, other, rest), jnp.where(odd, rest, other)], axis=2)
        rest = rest.reshape(16, *rest.shape[3:])
        return jnp.concatenate([self.join_rows(heard), self.join_rows(rest)], axis=0)

    def in_order(self, heard):
        odd, upper = self.z % 2 == 1, self.z >= 2
        low = [jnp.where(odd, heard[1], heard[0]), jnp.where(odd, heard[0], heard[1])]
        high = [jnp.where(odd, heard[3], heard[2]), jnp.where(odd, heard[2], heard[3])]
        return [jnp.where(upper, b, a) for a, b in zip(low, high)] + [
            jnp.where(upper, a, b) for a, b in zip(low, high)
        ]

    def gather_line(self, mine):
        heard = [mine] + [self.swap_z(mine, bits) for bits in (1, 2, 3)]
        return jnp.concatenate(self.in_order(heard), axis=0)

    def gather_near(self, quarter):
        return [quarter, self.swap_x(quarter), self.swap_y(quarter)]

    def gather_far(self, pieces):
        half = pieces[0].shape[0] // 2
        return [self.swap_y(pieces[1][:half]), self.swap_x(pieces[2][half:])]

    def gather_core(self, pieces):
        return [self.swap_core(piece) for piece in pieces]

    def scatter_core(self, pairs, after=()):
        *parts, partner = weight_grad(pairs, self.places, after=after)
        return [*parts, self.swap_core(partner)]

    def scatter_near(self, parts):
        own, for_x, for_y, far_one, far_two, heard = parts
        rows, half = own.shape[0], far_one.shape[0]
        far_one = (wide(far_one) + wide(heard[3 * rows : 3 * rows + half])).astype(jnp.bfloat16)
        far_two = (wide(far_two) + wide(heard[3 * rows + half :])).astype(jnp.bfloat16)
        return [own, for_x, for_y, heard, self.swap_x(far_one), self.swap_y(far_two)]

    def scatter_far(self, parts):
        own, for_x, for_y, heard, add_y, add_x = parts
        rows, half = own.shape[0], add_y.shape[0]
        heard_x, heard_y = wide(heard[rows : 2 * rows]), wide(heard[2 * rows : 3 * rows])
        for_x, for_y = wide(for_x) + heard_x, wide(for_y) + heard_y
        for_y = jnp.concatenate([for_y[:half] + wide(add_y), for_y[half:]], axis=0)
        for_x = jnp.concatenate([for_x[:half], for_x[half:] + wide(add_x)], axis=0)
        return [
            own,
            heard[:rows],
            self.swap_x(for_x.astype(jnp.bfloat16)),
            self.swap_y(for_y.astype(jnp.bfloat16)),
        ]

    def scatter_half(self, parts):
        quarter = sum(wide(part) for part in parts).astype(jnp.bfloat16)
        half, upper = quarter.shape[0] // 2, self.z // 2
        send = lax.dynamic_slice_in_dim(quarter, (1 - upper) * half, half, axis=0)
        return [lax.dynamic_slice_in_dim(quarter, upper * half, half, axis=0), self.swap_z(send, 2)]

    def scatter_slab(self, parts):
        both = wide(parts[0]) + wide(parts[1])
        slab, odd = both.shape[0] // 2, self.z % 2
        send = lax.dynamic_slice_in_dim(both, (1 - odd) * slab, slab, axis=0).astype(jnp.bfloat16)
        return [lax.dynamic_slice_in_dim(both, odd * slab, slab, axis=0), self.swap_z(send, 1)]

    def scatter_line(self, parts):
        quarter = sum(wide(part) for part in parts).astype(jnp.bfloat16)
        slab = quarter.shape[0] // 4

        def slab_of(bits):
            return lax.dynamic_slice_in_dim(quarter, (self.z ^ bits) * slab, slab, axis=0)

        return [slab_of(0)] + [self.swap_z(slab_of(bits), bits) for bits in (1, 2, 3)]

    def scatter_end(self, parts):
        total = wide(parts[0])
        for part in parts[1:]:
            total = total + wide(part)
        return total.astype(jnp.bfloat16)

    def total_step(self, part, kind):
        swaps = {
            "core": self.swap_core,
            "x": self.swap_x,
            "y": self.swap_y,
            "near z": lambda value: self.swap_z(value, 1),
            "far z": lambda value: self.swap_z(value, 2),
        }
        return part + swaps[kind](part)


def mesh_plan(shard_count, replica_count):
    kind = BlockMesh if (shard_count, replica_count) == (2, 16) else WholeMesh
    return kind(shard_count, replica_count)


def on_device(
    tokens,
    cotangent,
    segment_ids,
    owners,
    master,
    moment_one,
    moment_two,
    vectors,
    vector_one,
    vector_two,
):
    replica_count = lax.axis_size("replica")
    replica_index = lax.axis_index("replica")
    shard_count = lax.axis_size("shard")
    slot_count, shard_rows, stripe = master.shape
    columns = 4 * D + 2 * FF
    stripe_count = columns // stripe
    slab = shard_rows // replica_count
    stripe_ids = jnp.arange(stripe_count, dtype=jnp.int32)
    earlier = (owners[None, :] == owners[:, None]) & (stripe_ids[None, :] < stripe_ids[:, None])
    slot_of = jnp.sum(earlier.astype(jnp.int32), axis=1)
    slot_place = owners * slot_count + slot_of
    places = jnp.arange(replica_count * slot_count, dtype=jnp.int32)
    matches = (slot_place[None, :] == places[:, None]).astype(jnp.int32)
    stripe_at = jnp.sum(matches * stripe_ids[None, :], axis=1).reshape(replica_count, slot_count)
    used = jnp.sum(matches, axis=1) > 0
    heavy = jnp.max(jnp.where(slot_of == slot_count - 1, owners, 0))

    plan = mesh_plan(shard_count, replica_count)
    halves = master.astype(jnp.bfloat16)
    mine = plan.spread(halves, owners, slot_of, slab).transpose(1, 0, 2).reshape(slab, columns)
    up_bias = vectors[8:].reshape(1, FF)
    length = segment_ids.shape[1]
    seg_row = segment_ids.reshape(1, length)
    seg_col = segment_ids.reshape(length, 1)
    places = plan.places
    qkv_bias = jnp.concatenate([vectors[0], jnp.zeros((D,), jnp.float32), vectors[1]])[None]

    near_qkv = plan.gather_near(plan.gather_line(mine[:, : 3 * D]))
    core_qkv = plan.gather_core(near_qkv[:1])
    line_up = plan.gather_line(gate(mine[:, 3 * D : 4 * D + FF], core_qkv))
    far_qkv = plan.gather_far(near_qkv)
    core_qkv = [*core_qkv, *plan.gather_core(near_qkv[1:])]
    w_qkv = [*near_qkv, *far_qkv, *core_qkv, *plan.gather_core(far_qkv)]
    projected = project(tokens, qkv_bias, w_qkv, places)
    near_up = plan.gather_near(gate(line_up, far_qkv))
    line_down = plan.gather_line(gate(mine[:, 4 * D + FF :], projected))
    done = attend(projected, seg_col, seg_row, 0, 2, None)
    far_up = plan.gather_far(gate(near_up, done))
    done = attend(projected, seg_col, seg_row, 2, 2, done, after=near_up[1:])
    done = attend(projected, seg_col, seg_row, 4, 2, done, after=far_up)
    core_up = plan.gather_core(gate([*near_up, *far_up], done))
    context, logs = attend(projected, seg_col, seg_row, 6, 2, done, after=(line_down,))
    near_down = plan.gather_near(gate(line_down, context))
    w_up = [*near_up, *far_up, *core_up]
    unit, spread, normed_low, *filled = out_up(context, tokens, vectors, up_bias, w_up, places, 2)
    far_down = plan.gather_far(gate(near_down, normed_low))
    core_down = plan.gather_core(gate(near_down, normed_low))
    active, slope = up_rest(normed_low, up_bias, w_up, places, 2, filled, after=near_down[1:])
    w_down = [*near_down, *far_down, *core_down, *plan.gather_core(gate(far_down, active))]
    output, second, grad_branch, grad_up, down_sums, up_terms = down_both(
        unit, cotangent, active, slope, vectors, w_down, places
    )
    core_down = plan.scatter_core([(grad_branch, active[None])])
    first, grad_attn, grad_context, up_sums = up_back(
        unit, spread, second, grad_up, vectors, w_up, places, after=core_down[:1]
    )
    near_down = plan.scatter_near(gate(core_down, grad_attn))
    core_up = plan.scatter_core([(normed_low, grad_up[None])], after=[grad_attn, core_down[-1]])

    def back(first_pair, half_first, earlier, after):
        return attend_back(
            projected, context, grad_context, logs, seg_col, seg_row, first_pair, 2, half_first, 4, earlier, after
        )

    far_down = plan.scatter_far(gate(near_down, core_up[0]))
    grads = back(0, 0, None, near_down[-2:] + core_up[:1])
    near_up = plan.scatter_near(gate(core_up, grads[0]))
    grad_one, sums_one = back(2, 0, grads, core_up[-1:])
    core_one = plan.scatter_core(
        [(context, grad_attn[None]), (tokens, grad_one)], after=far_down[-2:] + near_up[-2:]
    )
    half_down = plan.scatter_half(gate(far_down, core_one[0]))
    far_up = plan.scatter_far(gate(near_up, core_one[0]))
    grads = back(4, 4, None, core_one[:1])
    near_one = plan.scatter_near(core_one)
    grad_two, sums_two = back(6, 4, grads, far_up[-2:] + half_down[-1:] + core_one[-1:])
    half_up = plan.scatter_half(gate(far_up, grad_two))
    line_down = plan.scatter_slab(half_down)
    core_two = plan.scatter_core([(tokens, grad_two)], after=near_one[-2:] + line_down[-1:])
    far_one = plan.scatter_far(gate(near_one, grad_two))
    input_grad = input_back(first, grad_one, grad_two, w_qkv, places, after=core_two[:1])
    head_sums = jnp.concatenate([sums_one, sums_two], axis=0)
    vector_part = jnp.concatenate(
        [
            head_sums[:, 0].reshape(1, D),
            head_sums[:, 1].reshape(1, D),
            up_sums[:3],
            down_sums[:3],
            up_terms.reshape(FF // D, D),
        ],
        axis=0,
    )
    vector_part = plan.total_step(gate(vector_part, core_two[0]), "core")
    near_two = plan.scatter_near(gate(core_two, vector_part, input_grad))
    line_one = plan.scatter_line(gate(far_one, near_two[-2:], half_up[-1]))
    vector_part = plan.total_step(gate(vector_part, near_two[-1]), "x")
    far_two = plan.scatter_far(near_two)
    line_up = plan.scatter_slab(gate(half_up, far_two[-1]))
    line_two = plan.scatter_line(gate(far_two, vector_part))
    vector_part = plan.total_step(gate(vector_part, far_two[-1]), "y")
    down_sum = plan.scatter_end(line_down)
    up_sum = plan.scatter_end(line_up)
    one_sum = plan.scatter_end(line_one)
    vector_part = plan.total_step(vector_part, "near z")
    vector_grad = plan.total_step(vector_part, "far z")
    two_sum = gate(plan.scatter_end(line_two), vector_grad)
    half = D // 2
    out_sum, one_sum = one_sum[:, :D], one_sum[:, D:]
    qkv_sum = [part[:, k * half : (k + 1) * half] for k in range(3) for part in (one_sum, two_sum)]
    summed = jnp.concatenate([*qkv_sum, out_sum, up_sum, down_sum], axis=1)
    stripes = summed.reshape(slab, stripe_count, stripe).transpose(1, 0, 2)
    slot_grad = plan.collect(stripes, stripe_at, heavy)
    keep = lax.dynamic_slice(used, (replica_index * slot_count,), (slot_count,))[:, None, None]
    new_master, new_one, new_two = adamw(
        master, moment_one, moment_two, slot_grad.astype(jnp.float32), rate_matrix, decay_rate
    )
    new_master = jnp.where(keep, new_master, 0.0)
    new_one = jnp.where(keep, new_one, 0.0)
    new_two = jnp.where(keep, new_two, 0.0)
    new_vectors, new_vector_one, new_vector_two = adamw(
        vectors, vector_one, vector_two, vector_grad, rate_vector, 0.0
    )
    return (
        output,
        input_grad,
        new_master,
        new_master.astype(jnp.bfloat16),
        new_one,
        new_two,
        new_vectors,
        new_vector_one,
        new_vector_two,
    )


def solution(mesh):
    return jax.shard_map(
        on_device,
        mesh=mesh,
        in_specs=(
            P(BOTH, None),
            P(BOTH, None),
            P(BOTH, None),
            P(),
            P("replica", "shard", None),
            P("replica", "shard", None),
            P("replica", "shard", None),
            P(),
            P(),
            P(),
        ),
        out_specs=(
            P(BOTH, None),
            P(BOTH, None),
            P("replica", "shard", None),
            P("replica", "shard", None),
            P("replica", "shard", None),
            P("replica", "shard", None),
            P(),
            P(),
            P(),
        ),
        check_vma=False,
    )
```

time: 1410 us -> 539 us (0.38)
  waiting for transfers between devices: 720 us -> 99.5 us
  matrix products: 322 us -> 0 us
  Pallas kernels: 0 us -> 259 us
  local copies, waits for them, and re-layouts: 178 us -> 36.6 us
  starting transfers between devices: 0.12 us -> 90.6 us
  other arithmetic: 123 us -> 37 us
  blocking collectives: 41.2 us -> 0 us
    dot_general x60 -> x0, matrix products: 322 us -> none  [the longest x1 48.3 us: on_device(): jnp.dot(normed_low, w_up, preferred_element_type=jnp.float32) + up_bias]
    unnamed x4 -> x0, waiting for transfers between devices: 278 us -> none
    all_gather x1 -> x0, waiting for transfers between devices: 270 us -> none  [on_device(): gathered = lax.all_gather(halves, ('shard', 'replica'), axis=0, tiled=True)]
    pallas_call x0 -> x18, Pallas kernels: none -> 259 us  [kernel_call(): pl.pallas_call(body, grid_spec=pltpu.PrefetchScalarGridSpec(num_scalar_pr...]
    psum x1 -> x0, waiting for transfers between devices: 173 us -> none  [on_device(): summed = lax.psum(grad_shard, 'replica').astype(jnp.float32)]
    ppermute x0 -> x81, waiting for transfers between devices: none -> 97.3 us  [the longest x66 96.4 us: swap(): return lax.ppermute(array, 'replica', [(r, r ^ bits) for r in range(16)])]
    ppermute x0 -> x81, starting transfers between devices: none -> 79.3 us  [the longest x66 64.2 us: swap(): return lax.ppermute(array, 'replica', [(r, r ^ bits) for r in range(16)])]
    select_n x1 -> x0, local copies, waits for them, and re-layouts: 60.9 us -> none  [on_device(): picked = jnp.take(grouped, slot_place, axis=1)]
  transfers between devices with their start and end apart: 3 -> 83, of which waited for: 3 -> 24; matrix products, arithmetic and copies ran while one was open for 2% -> 7% of each run, Pallas kernels for 0% -> 38%
where the time goes in v1:
time: 539 us; the launch traced here: 530 us
  Pallas kernels  259 us (48%)
  waiting for transfers between devices  99.5 us (18%)
  starting transfers between devices  90.6 us (17%)
  other arithmetic  37 us (7%)
  local copies, waits for them, and re-layouts  36.6 us (7%)
  between operations  7.34 us (1%)
    pallas_call x18, Pallas kernels, kernel_call(): pl.pallas_call(body, grid_spec=pltpu.PrefetchScalarGridSpec(num_scalar_pr...  259 us
    ppermute x66, waiting for transfers between devices, swap(): return lax.ppermute(array, 'replica', [(r, r ^ bits) for r in range(16)])  96.4 us
    ppermute x66, starting transfers between devices, swap(): return lax.ppermute(array, 'replica', [(r, r ^ bits) for r in range(16)])  64.2 us
    unnamed x176, local copies, waits for them, and re-layouts  16.3 us
    ppermute x15, starting transfers between devices, swap_y(): return lax.ppermute(array, 'shard', [(0, 1), (1, 0)])  15.1 us
  transfers between devices with their start and end apart: 83, of which 24 were waited for; matrix products, arithmetic and copies ran while one was open for 7% of the time, Pallas kernels for 38%

profile of v1, /device:TPU:0, one launch (start us, length us, event | category | flops | bytes accessed | tf_op | source)
XLA Modules:
  0.0 529.6 jit_solution(4280328194927378937)
XLA Ops:
  0.7 2.2 convert_element_type.287
  4.6 7.0 %all-to-all-start = ((bf16[16,6,32,128]{3,2,1,0:T(8,128)(2,1)}), bf16[16,6,32,128]{3,2,1,0:T(8,128)(2,1)S(1)}, u32[]{:S(2)}, u32[]{:S(2)}) async-start(bf16[16,6,32,128]{3,2,1,0:T(8,128)(2,1)} %bitcast.10), calls=%async_computation | async-start | bytes 1572864 | tf_op jit(solution)/shard_map/all_to_all | solution.py:928
  14.6 2.0 collective-permute-start.1
  17.3 8.3 %collective-permute-done.1 = bf16[4,6,32,128]{3,2,1,0:T(8,128)(2,1)S(1)} collective-permute-done((bf16[4,6,32,128]{3,2,1,0:T(8,128)(2,1)S(1)}, bf16[4,6,32,128]{3,2,1,0:T(8,128)(2,1)S(1)}, u32[]{:S(2)}, u32[]{:S(2)}) %collective-permute-start.1) | collective-permute-done | bytes 196640 | tf_op jit(solution)/shard_map/ppermute | solution.py:901
  25.7 4.0 collective-permute-start.2
  31.9 4.8 collective-permute-done.3
  39.2 2.9 collective-permute-start.7
  42.1 5.3 %collective-permute-done.5 = bf16[32,3072]{1,0:T(8,128)(2,1)S(1)} collective-permute-done((bf16[32,3072]{1,0:T(8,128)(2,1)S(1)}, bf16[32,3072]{1,0:T(8,128)(2,1)S(1)}, u32[]{:S(2)}, u32[]{:S(2)}) %collective-permute-start.5) | collective-permute-done | bytes 196640 | tf_op jit(solution)/shard_map/ppermute | solution.py:901
  47.4 8.3 %collective-permute-done.6 = bf16[32,3072]{1,0:T(8,128)(2,1)S(1)} collective-permute-done((bf16[32,3072]{1,0:T(8,128)(2,1)S(1)}, bf16[32,3072]{1,0:T(8,128)(2,1)S(1)}, u32[]{:S(2)}, u32[]{:S(2)}) %collective-permute-start.6) | collective-permute-done | bytes 196640 | tf_op jit(solution)/shard_map/ppermute | solution.py:901
  59.1 1.6 collective-permute-start.20
  60.7 2.9 collective-permute-start.22
  63.5 12.5 %collective-permute-done.8.refs_4_.refs_6_ = bf16[128,3072]{1,0:T(8,128)(2,1)} collective-permute-done((bf16[128,3072]{1,0:T(8,128)(2,1)S(1)}, bf16[128,3072]{1,0:T(8,128)(2,1)}, u32[]{:S(2)}, u32[]{:S(2)}) %collective-permute-start.8) | collective-permute-done | bytes 786464 | tf_op jit(solution)/shard_map/ppermute | solution.py:901
  77.1 1.6 collective-permute-start.10
  81.2 6.6 %collective-permute-done.21 = bf16[32,5120]{1,0:T(8,128)(2,1)S(1)} collective-permute-done((bf16[32,5120]{1,0:T(8,128)(2,1)S(1)}, bf16[32,5120]{1,0:T(8,128)(2,1)S(1)}, u32[]{:S(2)}, u32[]{:S(2)}) %collective-permute-start.21) | collective-permute-done | bytes 327712 | tf_op jit(solution)/shard_map/ppermute | solution.py:901
  92.8 1.7 collective-permute-done.15.refs_11_.refs_13_
  99.4 12.3 %project.1.refs_0_.refs_1_.refs_2_.refs_3_.refs_4_.refs_5_.refs_6_ = bf16[1024,3072]{1,0:T(8,128)(2,1)} custom-call(s32[8]{0:T(128)} %concatenate.62.refs_0_, bf16[1024,1024]{1,0:T(8,128)(2,1)} %refs_4_.5, f32[1,3072]{1,0:T(1,128)} %bitcast.106, bf16[128,3072]{1,0:T(8,128)(2,1)} %copy-done.14, bf16[128,3072]{1,0:T(8,128)(2,1)} %collective-permute-done.8.refs_4_.refs_6_, ...), custom_call_target="tpu_custom_call" | custom-call | flops 402653184 | bytes 918272 | tf_op jit(solution)/shard_map/project/pallas_call | solution.py:98
  111.7 9.7 %attend.4 = (bf16[1024,1024]{1,0:T(8,128)(2,1)}, f32[8,8,1024]{2,1,0:T(8,128)}) custom-call(bf16[1024,3072]{1,0:T(8,128)(2,1)} %project.1.refs_0_.refs_1_.refs_2_.refs_3_.refs_4_.refs_5_.refs_6_, bf16[1024,3072]{1,0:T(8,128)(2,1)} %project.1.refs_0_.refs_1_.refs_2_.refs_3_.refs_4_.refs_5_.refs_6_, ...), custom_call_target="tpu_custom_call" | custom-call | flops 268435456 | bytes 1327616 | tf_op jit(solution)/shard_map/attend/pallas_call | solution.py:98
  121.5 1.6 collective-permute-start.25
  124.8 1.6 collective-permute-start.17
  126.3 2.9 collective-permute-start.19
  129.2 10.2 %attend.5 = (bf16[1024,1024]{1,0:T(8,128)(2,1)}, f32[8,8,1024]{2,1,0:T(8,128)}) custom-call(bf16[128,5120]{1,0:T(8,128)(2,1)} %copy-done, bf16[128,5120]{1,0:T(8,128)(2,1)} %copy-done.2, bf16[1024,3072]{1,0:T(8,128)(2,1)} %project.1.refs_0_.refs_1_.refs_2_.refs_3_.refs_4_.refs_5_.refs_6_, ...), custom_call_target="tpu_custom_call", output_to_operand_aliasing={{0}: (7, {}), {1}: (8, {})} | custom-call | flops 268435456 | bytes 1475072 | tf_op jit(solution)/shard_map/attend/pallas_call | solution.py:98
  140.8 9.8 %attend.6 = (bf16[1024,1024]{1,0:T(8,128)(2,1)}, f32[8,8,1024]{2,1,0:T(8,128)}) custom-call(bf16[64,5120]{1,0:T(8,128)(2,1)} %copy-done.11, bf16[64,5120]{1,0:T(8,128)(2,1)} %copy-done.12, bf16[1024,3072]{1,0:T(8,128)(2,1)} %project.1.refs_0_.refs_1_.refs_2_.refs_3_.refs_4_.refs_5_.refs_6_, ...), custom_call_target="tpu_custom_call", output_to_operand_aliasing={{0}: (7, {}), {1}: (8, {})} | custom-call | flops 268435456 | bytes 1475072 | tf_op jit(solution)/shard_map/attend/pallas_call | solution.py:98
  153.6 10.0 %attend.7 = (bf16[1024,1024]{1,0:T(8,128)(2,1)}, f32[8,8,1024]{2,1,0:T(8,128)}) custom-call(bf16[128,4096]{1,0:T(8,128)(2,1)} %pad_maximum_fusion.2.refs_0_.refs_6_, bf16[1024,3072]{1,0:T(8,128)(2,1)} %project.1.refs_0_.refs_1_.refs_2_.refs_3_.refs_4_.refs_5_.refs_6_, ...), custom_call_target="tpu_custom_call", output_to_operand_aliasing={{0}: (6, {}), {1}: (7, {})} | custom-call | flops 268435456 | bytes 1475072 | tf_op jit(solution)/shard_map/attend/pallas_call | solution.py:98
  168.7 18.0 %out_up.1 = (f32[1024,1024]{1,0:T(8,128)}, f32[1024,128]{1,0:T(8,128)}, bf16[1024,1024]{1,0:T(8,128)(2,1)}, bf16[1024,4096]{1,0:T(8,128)(2,1)}, bf16[1024,4096]{1,0:T(8,128)(2,1)}) custom-call(s32[8]{0:T(128)} %concatenate.62.refs_0_, f32[12,1024]{1,0:T(8,128)} %refs_2_.1, f32[1,4096]{1,0:T(1,128)} %bitcast.104, ...), custom_call_target="tpu_custom_call" | custom-call | flops 402653184 | bytes 2396160 | tf_op jit(solution)/shard_map/out_up/pallas_call | solution.py:98
  186.7 2.1 collective-permute-done.32.refs_1_.refs_7_
  193.9 12.7 %up_rest.1 = (bf16[1024,4096]{1,0:T(8,128)(2,1)}, bf16[1024,4096]{1,0:T(8,128)(2,1)}) custom-call(s32[8]{0:T(128)} %concatenate.62.refs_0_, bf16[128,4096]{1,0:T(8,128)(2,1)} %collective-permute-done.32.refs_1_.refs_7_, bf16[128,4096]{1,0:T(8,128)(2,1)} %collective-permute-done.33.refs_2_.refs_8_, ...), custom_call_target="tpu_custom_call", output_to_operand_aliasing={{0}: (15, {}), {1}: (16, {})} | custom-call | flops 268435456 | bytes 2884608 | tf_op jit(solution)/shard_map/up_rest/pallas_call | solution.py:98
  210.3 31.1 %down_both.1 = (bf16[1024,1024]{1,0:T(8,128)(2,1)}, f32[1024,1024]{1,0:T(8,128)}, bf16[1024,1024]{1,0:T(8,128)(2,1)}, bf16[1024,4096]{1,0:T(8,128)(2,1)}, f32[8,1024]{1,0:T(8,128)}, /*index=5*/f32[1,4096]{1,0:T(1,128)}) custom-call(s32[8]{0:T(128)} %concatenate.62.refs_0_, f32[12,1024]{1,0:T(8,128)} %refs_2_.1, ...), custom_call_target="tpu_custom_call" | custom-call | flops 1073741824 | bytes 3020800 | tf_op jit(solution)/shard_map/down_both/pallas_call | solution.py:98
  241.4 14.8 %weight_grad.4 = (bf16[128,4096]{1,0:T(8,128)(2,1)}, bf16[128,4096]{1,0:T(8,128)(2,1)}, bf16[128,4096]{1,0:T(8,128)(2,1)}, bf16[64,4096]{1,0:T(8,128)(2,1)}, bf1...) custom-call(s32[8]{0:T(128)} %concatenate.62.refs_0_, bf16[1024,1024]{1,0:T(8,128)(2,1)} %get-tuple-element.171.refs_1_, ...), custom_call_target="tpu_custom_call" | custom-call | flops 536870912 | bytes 1179648 | tf_op jit(solution)/shard_map/weight_grad/pallas_call | solution.py:98
  256.4 21.9 %up_back.1 = (f32[1024,1024]{1,0:T(8,128)}, bf16[1024,1024]{1,0:T(8,128)(2,1)}, bf16[1024,1024]{1,0:T(8,128)(2,1)}, f32[8,1024]{1,0:T(8,128)}) custom-call(s32[8]{0:T(128)} %concatenate.62.refs_0_, bf16[128,4096]{1,0:T(8,128)(2,1)} %get-tuple-element.212.refs_1_, f32[12,1024]{1,0:T(8,128)} %refs_2_.1, f32[1024,1024]{1,0:T(8,128)} %get-tuple-element.158.refs_2_.refs_3_, ...), custom_call_target="tpu_custom_call" | custom-call | flops 671088640 | bytes 2266112 | tf_op jit(solution)/shard_map/up_back/pallas_call | solution.py:98
  278.3 2.0 copy-done.4
  284.9 14.7 %weight_grad.5 = (bf16[128,4096]{1,0:T(8,128)(2,1)}, bf16[128,4096]{1,0:T(8,128)(2,1)}, bf16[128,4096]{1,0:T(8,128)(2,1)}, bf16[64,4096]{1,0:T(8,128)(2,1)}, bf1...) custom-call(s32[8]{0:T(128)} %concatenate.62.refs_0_, bf16[1024,1024]{1,0:T(8,128)(2,1)} %get-tuple-element.181.refs_1_, ...), custom_call_target="tpu_custom_call" | custom-call | flops 536870912 | bytes 1179648 | tf_op jit(solution)/shard_map/weight_grad/pallas_call | solution.py:98
  302.5 2.6 convert_add_fusion.2
  309.0 14.8 %attend_back.4 = (bf16[3,1024,512]{2,1,0:T(8,128)(2,1)}, f32[4,8,128]{2,1,0:T(8,128)}) custom-call(bf16[64,4096]{1,0:T(8,128)(2,1)} %copy-done.35, bf16[64,4096]{1,0:T(8,128)(2,1)} %copy-done.36, bf16[128,4096]{1,0:T(8,128)(2,1)} %get-tuple-element.252.refs_2_, bf16[1024,3072]{1,0:T(8,128)(2,1)} %project.1.refs_0_.refs_1_.refs_2_.refs_3_.refs_4_.refs_5_.refs_6_, ...), custom_call_target="tpu_custom_call" | custom-call | flops 671088640 | bytes 1656320 | tf_op jit(solution)/shard_map/attend_back/pallas_call | solution.py:98
  323.9 2.5 add_convert_fusion.3
  332.1 14.9 %attend_back.5 = (bf16[3,1024,512]{2,1,0:T(8,128)(2,1)}, f32[4,8,128]{2,1,0:T(8,128)}) custom-call(bf16[512,4096]{1,0:T(8,128)(2,1)} %collective-permute-done.46.refs_0_, bf16[1024,3072]{1,0:T(8,128)(2,1)} %project.1.refs_0_.refs_1_.refs_2_.refs_3_.refs_4_.refs_5_.refs_6_, ...), custom_call_target="tpu_custom_call", output_to_operand_aliasing={{0}: (9, {}), {1}: (10, {})} | custom-call | flops 671088640 | bytes 1853952 | tf_op jit(solution)/shard_map/attend_back/pallas_call | solution.py:98
  349.4 12.5 %weight_grad.6 = (bf16[128,2560]{1,0:T(8,128)(2,1)}, bf16[128,2560]{1,0:T(8,128)(2,1)}, bf16[128,2560]{1,0:T(8,128)(2,1)}, bf16[64,2560]{1,0:T(8,128)(2,1)}, bf1...) custom-call(s32[8]{0:T(128)} %concatenate.62.refs_0_, bf16[128,4096]{1,0:T(8,128)(2,1)} %copy-done.18, ...), custom_call_target="tpu_custom_call" | custom-call | flops 335544320 | bytes 917504 | tf_op jit(solution)/shard_map/weight_grad/pallas_call | solution.py:98
  363.8 2.3 convert_add_fusion
  371.9 15.2 %attend_back.6 = (bf16[3,1024,512]{2,1,0:T(8,128)(2,1)}, f32[4,8,128]{2,1,0:T(8,128)}) custom-call(bf16[128,2560]{1,0:T(8,128)(2,1)} %get-tuple-element.256.refs_0_, bf16[1024,3072]{1,0:T(8,128)(2,1)} %project.1.refs_0_.refs_1_.refs_2_.refs_3_.refs_4_.refs_5_.refs_6_, bf16[1024,3072]{1,0:T(8,128)(2,1)} %project.1.refs_0_.refs_1_.refs_2_.refs_3_.refs_4_.refs_5_.refs_6_, ...), custom_call_target="tpu_custom_call" | custom-call | flops 671088640 | bytes 1656320 | tf_op jit(solution)/shard_map/attend_back/pallas_call | solution.py:98
  387.0 7.2 %collective-permute-done.52.refs_2_ = bf16[64,4096]{1,0:T(8,128)(2,1)S(1)} collective-permute-done((bf16[64,4096]{1,0:T(8,128)(2,1)S(1)}, bf16[64,4096]{1,0:T(8,128)(2,1)S(1)}, u32[]{:S(2)}, u32[]{:S(2)}) %collective-permute-start.52) | collective-permute-done | bytes 524320 | tf_op jit(solution)/shard_map/ppermute | solution.py:901
  399.0 14.9 %attend_back.7 = (bf16[3,1024,512]{2,1,0:T(8,128)(2,1)}, f32[4,8,128]{2,1,0:T(8,128)}) custom-call(bf16[128,4096]{1,0:T(8,128)(2,1)} %copy-done.21, bf16[128,4096]{1,0:T(8,128)(2,1)} %copy-done.20, bf16[64,4096]{1,0:T(8,128)(2,1)} %copy-done.30, bf16[512,2560]{1,0:T(8,128)(2,1)} %copy-done.9, ...), custom_call_target="tpu_custom_call", output_to_operand_aliasing={{0}: (12, {}), {1}: (13, {})} | custom-call | flops 671088640 | bytes 1853952 | tf_op jit(solution)/shard_map/attend_back/pallas_call | solution.py:98
  413.9 2.2 add_convert_fusion
  417.1 2.6 collective-permute-start.62
  421.3 8.4 %weight_grad.7 = (bf16[128,1536]{1,0:T(8,128)(2,1)}, bf16[128,1536]{1,0:T(8,128)(2,1)}, bf16[128,1536]{1,0:T(8,128)(2,1)}, bf16[64,1536]{1,0:T(8,128)(2,1)}, bf1...) custom-call(s32[8]{0:T(128)} %concatenate.62.refs_0_, bf16[64,2560]{1,0:T(8,128)(2,1)} %copy-done.43, ...), custom_call_target="tpu_custom_call" | custom-call | flops 201326592 | bytes 524288 | tf_op jit(solution)/shard_map/weight_grad/pallas_call | solution.py:98
  434.3 12.5 %input_back.1 = bf16[1024,1024]{1,0:T(8,128)(2,1)} custom-call(s32[8]{0:T(128)} %concatenate.62.refs_0_, bf16[128,1536]{1,0:T(8,128)(2,1)} %get-tuple-element.264.refs_1_, f32[1024,1024]{1,0:T(8,128)} %get-tuple-element.228.refs_2_, bf16[3,1024,512]{2,1,0:T(8,128)(2,1)} %get-tuple-element.206.refs_8_.refs_3_, ...), custom_call_target="tpu_custom_call" | custom-call | flops 402653184 | bytes 1179648 | tf_op jit(solution)/shard_map/input_back/pallas_call | solution.py:98
  448.6 5.2 collective-permute-done.60
  456.1 2.6 collective-permute-start.64
  458.8 1.7 collective-permute-start.65
  461.6 2.2 collective-permute-done.63
  463.8 6.7 %collective-permute-done.64 = bf16[32,2560]{1,0:T(8,128)(2,1)S(1)} collective-permute-done((bf16[32,2560]{1,0:T(8,128)(2,1)S(1)}, bf16[32,2560]{1,0:T(8,128)(2,1)S(1)}, u32[]{:S(2)}, u32[]{:S(2)}) %collective-permute-start.64) | collective-permute-done | bytes 163872 | tf_op jit(solution)/shard_map/ppermute | solution.py:901
  470.7 1.6 collective-permute-start.72
  472.6 2.6 collective-permute-start.69
  475.6 2.0 collective-permute-start.71
  479.9 3.9 collective-permute-done.73
  483.9 3.0 collective-permute-start.74
  487.0 2.3 collective-permute-done.74
  490.6 1.6 gather_fusion.1
  493.0 1.9 collective-permute-start.76
  495.0 1.9 collective-permute-start.77
  497.5 4.3 all-to-all-start.1
  501.9 1.8 collective-permute-start.79
  503.7 11.6 %collective-permute-done.79 = bf16[4,6,32,128]{3,2,1,0:T(8,128)(2,1)S(1)} collective-permute-done((bf16[4,6,32,128]{3,2,1,0:T(8,128)(2,1)S(1)}, bf16[4,6,32,128]{3,2,1,0:T(8,128)(2,1)S(1)}, u32[]{:S(2)}, u32[]{:S(2)}) %collective-permute-start.79) | collective-permute-done | bytes 196640 | tf_op jit(solution)/shard_map/ppermute | solution.py:901
  515.5 1.6 collective-permute-done.80
  518.3 2.2 all-to-all-done.1
  521.9 7.6 %fusion.22 = (bf16[12,512,128]{2,1,0:T(8,128)(2,1)}, f32[12,512,128]{2,1,0:T(8,128)}, f32[12,512,128]{2,1,0:T(8,128)}, f32[12,512,128]{2,1,0:T(8,128)}) fusion(f32[12,512,128]{2,1,0:T(8,128)S(1)} %copy-done.5, f32[12,512,128]{2,1,0:T(8,128)} %param.16, bf16[6,512,128]{2,1,0:T(8,128)(2,1)S(1)} %bitcast.98, bf16[6,512,128]{2,1,0:T(8,128)(2,1)S(1)} %bitcast.99, ...), kind=kLoop, calls=%fused_computation.176 | loop fusion | flops 16515072 | bytes 22020108 | tf_op jit(solution)/shard_map/convert_element_type | solution.py:1191
  (422 shorter events, 94.0 us)
Async XLA Ops:
  3.1 11.4 %collective-permute-start = (bf16[4,2,6,32,128]{4,3,2,0,1:T(8,128)(2,1)S(1)}, bf16[4,2,6,32,128]{4,3,2,0,1:T(8,128)(2,1)S(1)}, u32[]{:S(2)}, u32[]{:S(2)}) collective-permute-start(bf16[4,2,6,32,128]{4,3,2,0,1:T(8,128)(2,1)S(1)} %select_bitcast_fusion.2), channel_id=1, source_target_pairs={{0,1},{1,0},{2,3},{3,2},{4,5},{5,4},{6,7},{7,6},{8,9},{9,8},{10,11... | collective-permute-start | bytes 1179656 | tf_op jit(solution)/shard_map/ppermute | solution.py:901
  4.6 32.2 %all-to-all-start = ((bf16[16,6,32,128]{3,2,1,0:T(8,128)(2,1)}), bf16[16,6,32,128]{3,2,1,0:T(8,128)(2,1)S(1)}, u32[]{:S(2)}, u32[]{:S(2)}) async-start(bf16[16,6,32,128]{3,2,1,0:T(8,128)(2,1)} %bitcast.10), calls=%async_computation | async-start | bytes 1572864 | tf_op jit(solution)/shard_map/all_to_all | solution.py:928
  14.6 11.0 %collective-permute-start.1 = (bf16[4,6,32,128]{3,2,1,0:T(8,128)(2,1)S(1)}, bf16[4,6,32,128]{3,2,1,0:T(8,128)(2,1)S(1)}, u32[]{:S(2)}, u32[]{:S(2)}) collective-permute-start(bf16[4,6,32,128]{3,2,1,0:T(8,128)(2,1)S(1)} %select_bitcast_fusion.5), channel_id=1, source_target_pairs={{0,2},{1,3},{2,0},{3,1},{4,6},{5,7},{6,4},{7,5},{8,10},{9,11},{10,... | collective-permute-start | bytes 589832 | tf_op jit(solution)/shard_map/ppermute | solution.py:901
  37.7 9.8 %collective-permute-start.5 = (bf16[32,3072]{1,0:T(8,128)(2,1)S(1)}, bf16[32,3072]{1,0:T(8,128)(2,1)S(1)}, u32[]{:S(2)}, u32[]{:S(2)}) collective-permute-start(bf16[32,3072]{1,0:T(8,128)(2,1)S(1)} %slice.301), channel_id=1, source_target_pairs={{0,12},{1,13},{2,14},{3,15},{4,8},{5,9},{6,10},{7,11},{8,4},{9,5},... | collective-permute-start | bytes 589832 | tf_op jit(solution)/shard_map/ppermute | solution.py:901
  39.2 16.6 %collective-permute-start.6 = (bf16[32,3072]{1,0:T(8,128)(2,1)S(1)}, bf16[32,3072]{1,0:T(8,128)(2,1)S(1)}, u32[]{:S(2)}, u32[]{:S(2)}) collective-permute-start(bf16[32,3072]{1,0:T(8,128)(2,1)S(1)} %slice.301), channel_id=1, source_target_pairs={{0,8},{1,9},{2,10},{3,11},{4,12},{5,13},{6,14},{7,15},{8,0},{9,1},... | collective-permute-start | bytes 589832 | tf_op jit(solution)/shard_map/ppermute | solution.py:901
  39.2 16.6 %collective-permute-start.7 = (bf16[32,3072]{1,0:T(8,128)(2,1)S(1)}, bf16[32,3072]{1,0:T(8,128)(2,1)S(1)}, u32[]{:S(2)}, u32[]{:S(2)}) collective-permute-start(bf16[32,3072]{1,0:T(8,128)(2,1)S(1)} %slice.301), channel_id=1, source_target_pairs={{0,4},{1,5},{2,6},{3,7},{4,0},{5,1},{6,2},{7,3},{8,12},{9,13},{10,... | collective-permute-start | bytes 589832 | tf_op jit(solution)/shard_map/ppermute | solution.py:901
  56.0 20.1 %collective-permute-start.8 = (bf16[128,3072]{1,0:T(8,128)(2,1)S(1)}, bf16[128,3072]{1,0:T(8,128)(2,1)}, u32[]{:S(2)}, u32[]{:S(2)}) collective-permute-start(bf16[128,3072]{1,0:T(8,128)(2,1)S(1)} %pad_maximum_fusion.8.refs_3_.refs_5_), channel_id=1, source_target_pairs={{0,2},{1,3},{2,0},{3,1},{4,6},{5,7},{6,4},{7,5},{8,10},{9,11},{10,... | collective-permute-start | bytes 2359304 | tf_op jit(solution)/shard_map/ppermute | solution.py:901
  57.5 21.1 %collective-permute-start.9 = (bf16[128,3072]{1,0:T(8,128)(2,1)S(1)}, bf16[128,3072]{1,0:T(8,128)(2,1)}, u32[]{:S(2)}, u32[]{:S(2)}) collective-permute-start(bf16[128,3072]{1,0:T(8,128)(2,1)S(1)} %pad_maximum_fusion.8.refs_3_.refs_5_), channel_id=1, source_target_pairs={{0,16},{16,0},{1,17},{17,1},{2,18},{18,2},{3,19},{19,3},{4,20},{20... | collective-permute-start | bytes 2359304 | tf_op jit(solution)/shard_map/ppermute | solution.py:910
  59.1 22.1 %collective-permute-start.20 = (bf16[32,5120]{1,0:T(8,128)(2,1)S(1)}, bf16[32,5120]{1,0:T(8,128)(2,1)S(1)}, u32[]{:S(2)}, u32[]{:S(2)}) collective-permute-start(bf16[32,5120]{1,0:T(8,128)(2,1)S(1)} %slice.304), channel_id=1, source_target_pairs={{0,12},{1,13},{2,14},{3,15},{4,8},{5,9},{6,10},{7,11},{8,4},{9,5},... | collective-permute-start | bytes 983048 | tf_op jit(solution)/shard_map/ppermute | solution.py:901
  60.6 27.2 %collective-permute-start.21 = (bf16[32,5120]{1,0:T(8,128)(2,1)S(1)}, bf16[32,5120]{1,0:T(8,128)(2,1)S(1)}, u32[]{:S(2)}, u32[]{:S(2)}) collective-permute-start(bf16[32,5120]{1,0:T(8,128)(2,1)S(1)} %slice.304), channel_id=1, source_target_pairs={{0,8},{1,9},{2,10},{3,11},{4,12},{5,13},{6,14},{7,15},{8,0},{9,1},... | collective-permute-start | bytes 983048 | tf_op jit(solution)/shard_map/ppermute | solution.py:901
  60.7 27.2 %collective-permute-start.22 = (bf16[32,5120]{1,0:T(8,128)(2,1)S(1)}, bf16[32,5120]{1,0:T(8,128)(2,1)S(1)}, u32[]{:S(2)}, u32[]{:S(2)}) collective-permute-start(bf16[32,5120]{1,0:T(8,128)(2,1)S(1)} %slice.304), channel_id=1, source_target_pairs={{0,4},{1,5},{2,6},{3,7},{4,0},{5,1},{6,2},{7,3},{8,12},{9,13},{10,... | collective-permute-start | bytes 983048 | tf_op jit(solution)/shard_map/ppermute | solution.py:901
  77.1 12.1 %collective-permute-start.10 = (bf16[64,3072]{1,0:T(8,128)(2,1)S(1)}, bf16[64,3072]{1,0:T(8,128)(2,1)S(1)}, u32[]{:S(2)}, u32[]{:S(2)}) collective-permute-start(bf16[64,3072]{1,0:T(8,128)(2,1)S(1)} %slice.302), channel_id=1, source_target_pairs={{0,16},{16,0},{1,17},{17,1},{2,18},{18,2},{3,19},{19,3},{4,20},{20... | collective-permute-start | bytes 1179656 | tf_op jit(solution)/shard_map/ppermute | solution.py:910
  79.7 10.6 %collective-permute-start.11 = (bf16[64,3072]{1,0:T(8,128)(2,1)S(1)}, bf16[64,3072]{1,0:T(8,128)(2,1)}, u32[]{:S(2)}, u32[]{:S(2)}) collective-permute-start(bf16[64,3072]{1,0:T(8,128)(2,1)S(1)} %slice.303), channel_id=1, source_target_pairs={{0,2},{1,3},{2,0},{3,1},{4,6},{5,7},{6,4},{7,5},{8,10},{9,11},{10,... | collective-permute-start | bytes 1179656 | tf_op jit(solution)/shard_map/ppermute | solution.py:901
  90.3 31.2 %collective-permute-start.23 = (bf16[128,5120]{1,0:T(8,128)(2,1)}, bf16[128,5120]{1,0:T(8,128)(2,1)S(1)}, u32[]{:S(2)}, u32[]{:S(2)}) collective-permute-start(bf16[128,5120]{1,0:T(8,128)(2,1)} %pad_maximum_fusion.1.refs_5_.refs_7_), channel_id=1, source_target_pairs={{0,2},{1,3},{2,0},{3,1},{4,6},{5,7},{6,4},{7,5},{8,10},{9,11},{10,... | collective-permute-start | bytes 3932168 | tf_op jit(solution)/shard_map/ppermute | solution.py:901
  91.7 29.7 %collective-permute-start.24 = (bf16[128,5120]{1,0:T(8,128)(2,1)}, bf16[128,5120]{1,0:T(8,128)(2,1)S(1)}, u32[]{:S(2)}, u32[]{:S(2)}) collective-permute-start(bf16[128,5120]{1,0:T(8,128)(2,1)} %pad_maximum_fusion.1.refs_5_.refs_7_), channel_id=1, source_target_pairs={{0,16},{16,0},{1,17},{17,1},{2,18},{18,2},{3,19},{19,3},{4,20},{20... | collective-permute-start | bytes 3932168 | tf_op jit(solution)/shard_map/ppermute | solution.py:910
  121.5 17.9 %collective-permute-start.25 = (bf16[64,5120]{1,0:T(8,128)(2,1)S(1)}, bf16[64,5120]{1,0:T(8,128)(2,1)S(1)}, u32[]{:S(2)}, u32[]{:S(2)}) collective-permute-start(bf16[64,5120]{1,0:T(8,128)(2,1)S(1)} %slice.234), channel_id=1, source_target_pairs={{0,16},{16,0},{1,17},{17,1},{2,18},{18,2},{3,19},{19,3},{4,20},{20... | collective-permute-start | bytes 1966088 | tf_op jit(solution)/shard_map/ppermute | solution.py:910
  123.2 16.8 %collective-permute-start.26 = (bf16[64,5120]{1,0:T(8,128)(2,1)S(1)}, bf16[64,5120]{1,0:T(8,128)(2,1)S(1)}, u32[]{:S(2)}, u32[]{:S(2)}) collective-permute-start(bf16[64,5120]{1,0:T(8,128)(2,1)S(1)} %slice.235), channel_id=1, source_target_pairs={{0,2},{1,3},{2,0},{3,1},{4,6},{5,7},{6,4},{7,5},{8,10},{9,11},{10,... | collective-permute-start | bytes 1966088 | tf_op jit(solution)/shard_map/ppermute | solution.py:901
  124.8 26.4 %collective-permute-start.17 = (bf16[32,4096]{1,0:T(8,128)(2,1)S(1)}, bf16[32,4096]{1,0:T(8,128)(2,1)S(1)}, u32[]{:S(2)}, u32[]{:S(2)}) collective-permute-start(bf16[32,4096]{1,0:T(8,128)(2,1)S(1)} %slice.300), channel_id=1, source_target_pairs={{0,12},{1,13},{2,14},{3,15},{4,8},{5,9},{6,10},{7,11},{8,4},{9,5},... | collective-permute-start | bytes 786440 | tf_op jit(solution)/shard_map/ppermute | solution.py:901
  126.3 24.9 %collective-permute-start.18 = (bf16[32,4096]{1,0:T(8,128)(2,1)S(1)}, bf16[32,4096]{1,0:T(8,128)(2,1)S(1)}, u32[]{:S(2)}, u32[]{:S(2)}) collective-permute-start(bf16[32,4096]{1,0:T(8,128)(2,1)S(1)} %slice.300), channel_id=1, source_target_pairs={{0,8},{1,9},{2,10},{3,11},{4,12},{5,13},{6,14},{7,15},{8,0},{9,1},... | collective-permute-start | bytes 786440 | tf_op jit(solution)/shard_map/ppermute | solution.py:901
  126.3 24.9 %collective-permute-start.19 = (bf16[32,4096]{1,0:T(8,128)(2,1)S(1)}, bf16[32,4096]{1,0:T(8,128)(2,1)S(1)}, u32[]{:S(2)}, u32[]{:S(2)}) collective-permute-start(bf16[32,4096]{1,0:T(8,128)(2,1)S(1)} %slice.300), channel_id=1, source_target_pairs={{0,4},{1,5},{2,6},{3,7},{4,0},{5,1},{6,2},{7,3},{8,12},{9,13},{10,... | collective-permute-start | bytes 786440 | tf_op jit(solution)/shard_map/ppermute | solution.py:901
  150.7 12.9 %collective-permute-start.30 = (bf16[64,5120]{1,0:T(8,128)(2,1)}, bf16[64,5120]{1,0:T(8,128)(2,1)}, u32[]{:S(2)}, u32[]{:S(2)}) collective-permute-start(bf16[64,5120]{1,0:T(8,128)(2,1)} %copy-done.11), channel_id=1, source_target_pairs={{0,1},{1,0},{2,3},{3,2},{4,5},{5,4},{6,7},{7,6},{8,9},{9,8},{10,11... | collective-permute-start | bytes 1966088 | tf_op jit(solution)/shard_map/ppermute | solution.py:901
  150.7 14.1 %collective-permute-start.31 = (bf16[64,5120]{1,0:T(8,128)(2,1)}, bf16[64,5120]{1,0:T(8,128)(2,1)}, u32[]{:S(2)}, u32[]{:S(2)}) collective-permute-start(bf16[64,5120]{1,0:T(8,128)(2,1)} %copy-done.12), channel_id=1, source_target_pairs={{0,1},{1,0},{2,3},{3,2},{4,5},{5,4},{6,7},{7,6},{8,9},{9,8},{10,11... | collective-permute-start | bytes 1966088 | tf_op jit(solution)/shard_map/ppermute | solution.py:901
  151.3 15.3 %collective-permute-start.27 = (bf16[128,5120]{1,0:T(8,128)(2,1)}, bf16[128,5120]{1,0:T(8,128)(2,1)S(1)}, u32[]{:S(2)}, u32[]{:S(2)}) collective-permute-start(bf16[128,5120]{1,0:T(8,128)(2,1)} %pad_maximum_fusion.1.refs_5_.refs_7_), channel_id=1, source_target_pairs={{0,1},{1,0},{2,3},{3,2},{4,5},{5,4},{6,7},{7,6},{8,9},{9,8},{10,11... | collective-permute-start | bytes 3932168 | tf_op jit(solution)/shard_map/ppermute | solution.py:901
  152.0 14.7 %collective-permute-start.28 = (bf16[128,5120]{1,0:T(8,128)(2,1)S(1)}, bf16[128,5120]{1,0:T(8,128)(2,1)S(1)}, u32[]{:S(2)}, u32[]{:S(2)}) collective-permute-start(bf16[128,5120]{1,0:T(8,128)(2,1)S(1)} %copy-done.1), channel_id=1, source_target_pairs={{0,1},{1,0},{2,3},{3,2},{4,5},{5,4},{6,7},{7,6},{8,9},{9,8},{10,11... | collective-permute-start | bytes 3932168 | tf_op jit(solution)/shard_map/ppermute | solution.py:901
  152.0 14.7 %collective-permute-start.29 = (bf16[128,5120]{1,0:T(8,128)(2,1)S(1)}, bf16[128,5120]{1,0:T(8,128)(2,1)S(1)}, u32[]{:S(2)}, u32[]{:S(2)}) collective-permute-start(bf16[128,5120]{1,0:T(8,128)(2,1)S(1)} %copy-done.3), channel_id=1, source_target_pairs={{0,1},{1,0},{2,3},{3,2},{4,5},{5,4},{6,7},{7,6},{8,9},{9,8},{10,11... | collective-permute-start | bytes 3932168 | tf_op jit(solution)/shard_map/ppermute | solution.py:901
  163.6 25.2 %collective-permute-start.32 = (bf16[128,4096]{1,0:T(8,128)(2,1)S(1)}, bf16[128,4096]{1,0:T(8,128)(2,1)}, u32[]{:S(2)}, u32[]{:S(2)}) collective-permute-start(bf16[128,4096]{1,0:T(8,128)(2,1)S(1)} %copy-done.13), channel_id=1, source_target_pairs={{0,2},{1,3},{2,0},{3,1},{4,6},{5,7},{6,4},{7,5},{8,10},{9,11},{10,... | collective-permute-start | bytes 3145736 | tf_op jit(solution)/shard_map/ppermute | solution.py:901
  164.8 24.9 %collective-permute-start.33 = (bf16[128,4096]{1,0:T(8,128)(2,1)S(1)}, bf16[128,4096]{1,0:T(8,128)(2,1)}, u32[]{:S(2)}, u32[]{:S(2)}) collective-permute-start(bf16[128,4096]{1,0:T(8,128)(2,1)S(1)} %copy-done.13), channel_id=1, source_target_pairs={{0,16},{16,0},{1,17},{17,1},{2,18},{18,2},{3,19},{19,3},{4,20},{20... | collective-permute-start | bytes 3145736 | tf_op jit(solution)/shard_map/ppermute | solution.py:910
  190.8 15.8 %collective-permute-start.34 = (bf16[64,4096]{1,0:T(8,128)(2,1)S(1)}, bf16[64,4096]{1,0:T(8,128)(2,1)S(1)}, u32[]{:S(2)}, u32[]{:S(2)}) collective-permute-start(bf16[64,4096]{1,0:T(8,128)(2,1)S(1)} %slice.236), channel_id=1, source_target_pairs={{0,16},{16,0},{1,17},{17,1},{2,18},{18,2},{3,19},{19,3},{4,20},{20... | collective-permute-start | bytes 1572872 | tf_op jit(solution)/shard_map/ppermute | solution.py:910
  192.4 14.2 %collective-permute-start.35 = (bf16[64,4096]{1,0:T(8,128)(2,1)S(1)}, bf16[64,4096]{1,0:T(8,128)(2,1)S(1)}, u32[]{:S(2)}, u32[]{:S(2)}) collective-permute-start(bf16[64,4096]{1,0:T(8,128)(2,1)S(1)} %slice.237), channel_id=1, source_target_pairs={{0,2},{1,3},{2,0},{3,1},{4,6},{5,7},{6,4},{7,5},{8,10},{9,11},{10,... | collective-permute-start | bytes 1572872 | tf_op jit(solution)/shard_map/ppermute | solution.py:901
  193.3 13.9 %collective-permute-start.36 = (bf16[128,4096]{1,0:T(8,128)(2,1)S(1)}, bf16[128,4096]{1,0:T(8,128)(2,1)S(1)}, u32[]{:S(2)}, u32[]{:S(2)}) collective-permute-start(bf16[128,4096]{1,0:T(8,128)(2,1)S(1)} %copy-done.13), channel_id=1, source_target_pairs={{0,1},{1,0},{2,3},{3,2},{4,5},{5,4},{6,7},{7,6},{8,9},{9,8},{10,11... | collective-permute-start | bytes 3145736 | tf_op jit(solution)/shard_map/ppermute | solution.py:901
  193.4 13.9 %collective-permute-start.37 = (bf16[128,4096]{1,0:T(8,128)(2,1)}, bf16[128,4096]{1,0:T(8,128)(2,1)S(1)}, u32[]{:S(2)}, u32[]{:S(2)}) collective-permute-start(bf16[128,4096]{1,0:T(8,128)(2,1)} %collective-permute-done.32.refs_1_.refs_7_), channel_id=1, source_target_pairs={{0,1},{1,0},{2,3},{3,2},{4,5},{5,4},{6,7},{7,6},{8,9},{9,8},{10,11... | collective-permute-start | bytes 3145736 | tf_op jit(solution)/shard_map/ppermute | solution.py:901
  193.9 13.4 %collective-permute-start.38 = (bf16[128,4096]{1,0:T(8,128)(2,1)}, bf16[128,4096]{1,0:T(8,128)(2,1)S(1)}, u32[]{:S(2)}, u32[]{:S(2)}) collective-permute-start(bf16[128,4096]{1,0:T(8,128)(2,1)} %collective-permute-done.33.refs_2_.refs_8_), channel_id=1, source_target_pairs={{0,1},{1,0},{2,3},{3,2},{4,5},{5,4},{6,7},{7,6},{8,9},{9,8},{10,11... | collective-permute-start | bytes 3145736 | tf_op jit(solution)/shard_map/ppermute | solution.py:901
  256.2 22.1 %collective-permute-start.41 = (bf16[512,4096]{1,0:T(8,128)(2,1)}, bf16[512,4096]{1,0:T(8,128)(2,1)S(1)}, u32[]{:S(2)}, u32[]{:S(2)}) collective-permute-start(bf16[512,4096]{1,0:T(8,128)(2,1)} %get-tuple-element.177), channel_id=1, source_target_pairs={{0,1},{1,0},{2,3},{3,2},{4,5},{5,4},{6,7},{7,6},{8,9},{9,8},{10,11... | collective-permute-start | bytes 12582920 | tf_op jit(solution)/shard_map/ppermute | solution.py:901
  281.5 21.0 %collective-permute-start.42 = (bf16[64,4096]{1,0:T(8,128)(2,1)}, bf16[64,4096]{1,0:T(8,128)(2,1)S(1)}, u32[]{:S(2)}, u32[]{:S(2)}) collective-permute-start(bf16[64,4096]{1,0:T(8,128)(2,1)} %get-tuple-element.292), channel_id=1, source_target_pairs={{0,2},{1,3},{2,0},{3,1},{4,6},{5,7},{6,4},{7,5},{8,10},{9,11},{10,... | collective-permute-start | bytes 1572872 | tf_op jit(solution)/shard_map/ppermute | solution.py:901
  282.6 19.9 %collective-permute-start.43 = (bf16[64,4096]{1,0:T(8,128)(2,1)}, bf16[64,4096]{1,0:T(8,128)(2,1)S(1)}, u32[]{:S(2)}, u32[]{:S(2)}) collective-permute-start(bf16[64,4096]{1,0:T(8,128)(2,1)} %get-tuple-element.291), channel_id=1, source_target_pairs={{0,16},{16,0},{1,17},{17,1},{2,18},{18,2},{3,19},{19,3},{4,20},{20... | collective-permute-start | bytes 1572872 | tf_op jit(solution)/shard_map/ppermute | solution.py:910
  299.7 24.2 %collective-permute-start.46 = (bf16[512,4096]{1,0:T(8,128)(2,1)}, bf16[512,4096]{1,0:T(8,128)(2,1)}, u32[]{:S(2)}, u32[]{:S(2)}) collective-permute-start(bf16[512,4096]{1,0:T(8,128)(2,1)} %get-tuple-element.198), channel_id=1, source_target_pairs={{0,1},{1,0},{2,3},{3,2},{4,5},{5,4},{6,7},{7,6},{8,9},{9,8},{10,11... | collective-permute-start | bytes 12582920 | tf_op jit(solution)/shard_map/ppermute | solution.py:901
  306.4 41.4 %collective-permute-start.45 = (bf16[128,4096]{1,0:T(8,128)(2,1)}, bf16[128,4096]{1,0:T(8,128)(2,1)S(1)}, u32[]{:S(2)}, u32[]{:S(2)}) collective-permute-start(bf16[128,4096]{1,0:T(8,128)(2,1)} %pad_maximum_fusion.4), channel_id=1, source_target_pairs={{0,16},{16,0},{1,17},{17,1},{2,18},{18,2},{3,19},{19,3},{4,20},{20... | collective-permute-start | bytes 3145736 | tf_op jit(solution)/shard_map/ppermute | solution.py:910
  308.1 39.6 %collective-permute-start.44 = (bf16[128,4096]{1,0:T(8,128)(2,1)}, bf16[128,4096]{1,0:T(8,128)(2,1)S(1)}, u32[]{:S(2)}, u32[]{:S(2)}) collective-permute-start(bf16[128,4096]{1,0:T(8,128)(2,1)} %pad_maximum_fusion.3), channel_id=1, source_target_pairs={{0,2},{1,3},{2,0},{3,1},{4,6},{5,7},{6,4},{7,5},{8,10},{9,11},{10,... | collective-permute-start | bytes 3145736 | tf_op jit(solution)/shard_map/ppermute | solution.py:901
  326.4 21.4 %collective-permute-start.47 = (bf16[64,4096]{1,0:T(8,128)(2,1)}, bf16[64,4096]{1,0:T(8,128)(2,1)S(1)}, u32[]{:S(2)}, u32[]{:S(2)}) collective-permute-start(bf16[64,4096]{1,0:T(8,128)(2,1)} %get-tuple-element.288), channel_id=1, source_target_pairs={{0,2},{1,3},{2,0},{3,1},{4,6},{5,7},{6,4},{7,5},{8,10},{9,11},{10,... | collective-permute-start | bytes 1572872 | tf_op jit(solution)/shard_map/ppermute | solution.py:901
  327.5 20.3 %collective-permute-start.48 = (bf16[64,4096]{1,0:T(8,128)(2,1)}, bf16[64,4096]{1,0:T(8,128)(2,1)S(1)}, u32[]{:S(2)}, u32[]{:S(2)}) collective-permute-start(bf16[64,4096]{1,0:T(8,128)(2,1)} %get-tuple-element.287), channel_id=1, source_target_pairs={{0,16},{16,0},{1,17},{17,1},{2,18},{18,2},{3,19},{19,3},{4,20},{20... | collective-permute-start | bytes 1572872 | tf_op jit(solution)/shard_map/ppermute | solution.py:910
  367.4 30.3 %collective-permute-start.55 = (bf16[128,4096]{1,0:T(8,128)(2,1)}, bf16[128,4096]{1,0:T(8,128)(2,1)S(1)}, u32[]{:S(2)}, u32[]{:S(2)}) collective-permute-start(bf16[128,4096]{1,0:T(8,128)(2,1)} %pad_maximum_fusion.6), channel_id=1, source_target_pairs={{0,16},{16,0},{1,17},{17,1},{2,18},{18,2},{3,19},{19,3},{4,20},{20... | collective-permute-start | bytes 3145736 | tf_op jit(solution)/shard_map/ppermute | solution.py:910
  369.4 24.8 %collective-permute-start.52 = (bf16[64,4096]{1,0:T(8,128)(2,1)S(1)}, bf16[64,4096]{1,0:T(8,128)(2,1)S(1)}, u32[]{:S(2)}, u32[]{:S(2)}) collective-permute-start(bf16[64,4096]{1,0:T(8,128)(2,1)S(1)} %constant_dynamic-slice_fusion.9), channel_id=1, source_target_pairs={{0,8},{1,9},{2,10},{3,11},{4,12},{5,13},{6,14},{7,15},{8,0},{9,1},... | collective-permute-start | bytes 1572872 | tf_op jit(solution)/shard_map/ppermute | solution.py:901
  369.6 25.7 %collective-permute-start.49 = (bf16[512,2560]{1,0:T(8,128)(2,1)}, bf16[512,2560]{1,0:T(8,128)(2,1)S(1)}, u32[]{:S(2)}, u32[]{:S(2)}) collective-permute-start(bf16[512,2560]{1,0:T(8,128)(2,1)} %get-tuple-element.208), channel_id=1, source_target_pairs={{0,1},{1,0},{2,3},{3,2},{4,5},{5,4},{6,7},{7,6},{8,9},{9,8},{10,11... | collective-permute-start | bytes 7864328 | tf_op jit(solution)/shard_map/ppermute | solution.py:901
  370.9 26.7 %collective-permute-start.54 = (bf16[128,4096]{1,0:T(8,128)(2,1)}, bf16[128,4096]{1,0:T(8,128)(2,1)S(1)}, u32[]{:S(2)}, u32[]{:S(2)}) collective-permute-start(bf16[128,4096]{1,0:T(8,128)(2,1)} %pad_maximum_fusion.5), channel_id=1, source_target_pairs={{0,2},{1,3},{2,0},{3,1},{4,6},{5,7},{6,4},{7,5},{8,10},{9,11},{10,... | collective-permute-start | bytes 3145736 | tf_op jit(solution)/shard_map/ppermute | solution.py:901
  395.3 24.5 %collective-permute-start.53 = (bf16[32,4096]{1,0:T(8,128)(2,1)}, bf16[32,4096]{1,0:T(8,128)(2,1)S(1)}, u32[]{:S(2)}, u32[]{:S(2)}) collective-permute-start(bf16[32,4096]{1,0:T(8,128)(2,1)} %dynamic-slice_convert_fusion.1), channel_id=1, source_target_pairs={{0,4},{1,5},{2,6},{3,7},{4,0},{5,1},{6,2},{7,3},{8,12},{9,13},{10,... | collective-permute-start | bytes 786440 | tf_op jit(solution)/shard_map/ppermute | solution.py:901
  396.5 23.3 %collective-permute-start.50 = (bf16[64,2560]{1,0:T(8,128)(2,1)}, bf16[64,2560]{1,0:T(8,128)(2,1)S(1)}, u32[]{:S(2)}, u32[]{:S(2)}) collective-permute-start(bf16[64,2560]{1,0:T(8,128)(2,1)} %get-tuple-element.296), channel_id=1, source_target_pairs={{0,2},{1,3},{2,0},{3,1},{4,6},{5,7},{6,4},{7,5},{8,10},{9,11},{10,... | collective-permute-start | bytes 983048 | tf_op jit(solution)/shard_map/ppermute | solution.py:901
  397.1 22.7 %collective-permute-start.51 = (bf16[64,2560]{1,0:T(8,128)(2,1)}, bf16[64,2560]{1,0:T(8,128)(2,1)S(1)}, u32[]{:S(2)}, u32[]{:S(2)}) collective-permute-start(bf16[64,2560]{1,0:T(8,128)(2,1)} %get-tuple-element.295), channel_id=1, source_target_pairs={{0,16},{16,0},{1,17},{17,1},{2,18},{18,2},{3,19},{19,3},{4,20},{20... | collective-permute-start | bytes 983048 | tf_op jit(solution)/shard_map/ppermute | solution.py:910
  417.1 38.5 %collective-permute-start.62 = (bf16[64,4096]{1,0:T(8,128)(2,1)}, bf16[64,4096]{1,0:T(8,128)(2,1)S(1)}, u32[]{:S(2)}, u32[]{:S(2)}) collective-permute-start(bf16[64,4096]{1,0:T(8,128)(2,1)} %get-tuple-element.312), channel_id=1, source_target_pairs={{0,8},{1,9},{2,10},{3,11},{4,12},{5,13},{6,14},{7,15},{8,0},{9,1},... | collective-permute-start | bytes 1572872 | tf_op jit(solution)/shard_map/ppermute | solution.py:901
  429.7 17.1 %collective-permute-start.59 = (f32[12,1024]{1,0:T(8,128)S(1)}, f32[12,1024]{1,0:T(8,128)S(1)}, u32[]{:S(2)}, u32[]{:S(2)}) collective-permute-start(f32[12,1024]{1,0:T(8,128)S(1)} %concatenate.75), channel_id=1, source_target_pairs={{0,1},{1,0},{2,3},{3,2},{4,5},{5,4},{6,7},{7,6},{8,9},{9,8},{10,11... | collective-permute-start | bytes 147464 | tf_op jit(solution)/shard_map/ppermute | solution.py:901
  429.7 17.1 %collective-permute-start.58 = (bf16[512,1536]{1,0:T(8,128)(2,1)}, bf16[512,1536]{1,0:T(8,128)(2,1)S(1)}, u32[]{:S(2)}, u32[]{:S(2)}) collective-permute-start(bf16[512,1536]{1,0:T(8,128)(2,1)} %get-tuple-element.241), channel_id=1, source_target_pairs={{0,1},{1,0},{2,3},{3,2},{4,5},{5,4},{6,7},{7,6},{8,9},{9,8},{10,11... | collective-permute-start | bytes 4718600 | tf_op jit(solution)/shard_map/ppermute | solution.py:901
  431.4 24.2 %collective-permute-start.57 = (bf16[128,2560]{1,0:T(8,128)(2,1)S(1)}, bf16[128,2560]{1,0:T(8,128)(2,1)S(1)}, u32[]{:S(2)}, u32[]{:S(2)}) collective-permute-start(bf16[128,2560]{1,0:T(8,128)(2,1)S(1)} %pad_maximum_fusion.10), channel_id=1, source_target_pairs={{0,16},{16,0},{1,17},{17,1},{2,18},{18,2},{3,19},{19,3},{4,20},{20... | collective-permute-start | bytes 1966088 | tf_op jit(solution)/shard_map/ppermute | solution.py:910
  433.1 22.5 %collective-permute-start.56 = (bf16[128,2560]{1,0:T(8,128)(2,1)S(1)}, bf16[128,2560]{1,0:T(8,128)(2,1)S(1)}, u32[]{:S(2)}, u32[]{:S(2)}) collective-permute-start(bf16[128,2560]{1,0:T(8,128)(2,1)S(1)} %pad_maximum_fusion.9), channel_id=1, source_target_pairs={{0,2},{1,3},{2,0},{3,1},{4,6},{5,7},{6,4},{7,5},{8,10},{9,11},{10,... | collective-permute-start | bytes 1966088 | tf_op jit(solution)/shard_map/ppermute | solution.py:901
  453.9 16.8 %collective-permute-start.67 = (bf16[128,1536]{1,0:T(8,128)(2,1)S(1)}, bf16[128,1536]{1,0:T(8,128)(2,1)S(1)}, u32[]{:S(2)}, u32[]{:S(2)}) collective-permute-start(bf16[128,1536]{1,0:T(8,128)(2,1)S(1)} %pad_maximum_fusion.12), channel_id=1, source_target_pairs={{0,16},{16,0},{1,17},{17,1},{2,18},{18,2},{3,19},{19,3},{4,20},{20... | collective-permute-start | bytes 1179656 | tf_op jit(solution)/shard_map/ppermute | solution.py:910
  456.0 7.8 %collective-permute-start.63 = (bf16[32,2560]{1,0:T(8,128)(2,1)S(1)}, bf16[32,2560]{1,0:T(8,128)(2,1)S(1)}, u32[]{:S(2)}, u32[]{:S(2)}) collective-permute-start(bf16[32,2560]{1,0:T(8,128)(2,1)S(1)} %get-tuple-element.319), channel_id=1, source_target_pairs={{0,4},{1,5},{2,6},{3,7},{4,0},{5,1},{6,2},{7,3},{8,12},{9,13},{10,... | collective-permute-start | bytes 491528 | tf_op jit(solution)/shard_map/ppermute | solution.py:901
  456.1 14.5 %collective-permute-start.64 = (bf16[32,2560]{1,0:T(8,128)(2,1)S(1)}, bf16[32,2560]{1,0:T(8,128)(2,1)S(1)}, u32[]{:S(2)}, u32[]{:S(2)}) collective-permute-start(bf16[32,2560]{1,0:T(8,128)(2,1)S(1)} %get-tuple-element.321), channel_id=1, source_target_pairs={{0,8},{1,9},{2,10},{3,11},{4,12},{5,13},{6,14},{7,15},{8,0},{9,1},... | collective-permute-start | bytes 491528 | tf_op jit(solution)/shard_map/ppermute | solution.py:901
  458.8 11.8 %collective-permute-start.65 = (bf16[32,2560]{1,0:T(8,128)(2,1)S(1)}, bf16[32,2560]{1,0:T(8,128)(2,1)S(1)}, u32[]{:S(2)}, u32[]{:S(2)}) collective-permute-start(bf16[32,2560]{1,0:T(8,128)(2,1)S(1)} %get-tuple-element.320), channel_id=1, source_target_pairs={{0,12},{1,13},{2,14},{3,15},{4,8},{5,9},{6,10},{7,11},{8,4},{9,5},... | collective-permute-start | bytes 491528 | tf_op jit(solution)/shard_map/ppermute | solution.py:901
  460.6 11.7 %collective-permute-start.66 = (bf16[128,1536]{1,0:T(8,128)(2,1)S(1)}, bf16[128,1536]{1,0:T(8,128)(2,1)S(1)}, u32[]{:S(2)}, u32[]{:S(2)}) collective-permute-start(bf16[128,1536]{1,0:T(8,128)(2,1)S(1)} %pad_maximum_fusion.11), channel_id=1, source_target_pairs={{0,2},{1,3},{2,0},{3,1},{4,6},{5,7},{6,4},{7,5},{8,10},{9,11},{10,... | collective-permute-start | bytes 1179656 | tf_op jit(solution)/shard_map/ppermute | solution.py:901
  472.6 14.3 %collective-permute-start.69 = (bf16[32,1536]{1,0:T(8,128)(2,1)S(1)}, bf16[32,1536]{1,0:T(8,128)(2,1)S(1)}, u32[]{:S(2)}, u32[]{:S(2)}) collective-permute-start(bf16[32,1536]{1,0:T(8,128)(2,1)S(1)} %get-tuple-element.324), channel_id=1, source_target_pairs={{0,4},{1,5},{2,6},{3,7},{4,0},{5,1},{6,2},{7,3},{8,12},{9,13},{10,... | collective-permute-start | bytes 294920 | tf_op jit(solution)/shard_map/ppermute | solution.py:901
  475.1 11.8 %collective-permute-start.70 = (bf16[32,1536]{1,0:T(8,128)(2,1)S(1)}, bf16[32,1536]{1,0:T(8,128)(2,1)S(1)}, u32[]{:S(2)}, u32[]{:S(2)}) collective-permute-start(bf16[32,1536]{1,0:T(8,128)(2,1)S(1)} %get-tuple-element.326), channel_id=1, source_target_pairs={{0,8},{1,9},{2,10},{3,11},{4,12},{5,13},{6,14},{7,15},{8,0},{9,1},... | collective-permute-start | bytes 294920 | tf_op jit(solution)/shard_map/ppermute | solution.py:901
  475.6 11.3 %collective-permute-start.71 = (bf16[32,1536]{1,0:T(8,128)(2,1)S(1)}, bf16[32,1536]{1,0:T(8,128)(2,1)S(1)}, u32[]{:S(2)}, u32[]{:S(2)}) collective-permute-start(bf16[32,1536]{1,0:T(8,128)(2,1)S(1)} %get-tuple-element.325), channel_id=1, source_target_pairs={{0,12},{1,13},{2,14},{3,15},{4,8},{5,9},{6,10},{7,11},{8,4},{9,5},... | collective-permute-start | bytes 294920 | tf_op jit(solution)/shard_map/ppermute | solution.py:901
  478.9 11.5 %collective-permute-start.75 = (bf16[32,4096]{1,0:T(8,128)(2,1)S(1)}, bf16[32,4096]{1,0:T(8,128)(2,1)S(1)}, u32[]{:S(2)}, u32[]{:S(2)}) collective-permute-start(bf16[32,4096]{1,0:T(8,128)(2,1)S(1)} %dynamic-slice_convert_fusion), channel_id=1, source_target_pairs={{0,4},{1,5},{2,6},{3,7},{4,0},{5,1},{6,2},{7,3},{8,12},{9,13},{10,... | collective-permute-start | bytes 786440 | tf_op jit(solution)/shard_map/ppermute | solution.py:901
  493.0 8.7 %collective-permute-start.76 = (bf16[6,32,128]{2,1,0:T(8,128)(2,1)S(1)}, bf16[6,32,128]{2,1,0:T(8,128)(2,1)S(1)}, u32[]{:S(2)}, u32[]{:S(2)}) collective-permute-start(bf16[6,32,128]{2,1,0:T(8,128)(2,1)S(1)} %gather_fusion.2), channel_id=1, source_target_pairs={{0,12},{1,13},{2,14},{3,15},{4,8},{5,9},{6,10},{7,11},{8,4},{9,5},... | collective-permute-start | bytes 147464 | tf_op jit(solution)/shard_map/ppermute | solution.py:901
  497.5 23.0 %all-to-all-start.1 = ((bf16[16,6,32,128]{3,2,1,0:T(8,128)(2,1)}), bf16[16,6,32,128]{3,2,1,0:T(8,128)(2,1)}, u32[]{:S(2)}, u32[]{:S(2)}) async-start(bf16[16,6,32,128]{3,2,1,0:T(8,128)(2,1)} %bitcast.33), calls=%async_computation.1 | async-start | bytes 1572864 | tf_op jit(solution)/shard_map/all_to_all | solution.py:952
  501.9 13.4 %collective-permute-start.79 = (bf16[4,6,32,128]{3,2,1,0:T(8,128)(2,1)S(1)}, bf16[4,6,32,128]{3,2,1,0:T(8,128)(2,1)S(1)}, u32[]{:S(2)}, u32[]{:S(2)}) collective-permute-start(bf16[4,6,32,128]{3,2,1,0:T(8,128)(2,1)S(1)} %pad_maximum_fusion.14), channel_id=1, source_target_pairs={{0,2},{1,3},{2,0},{3,1},{4,6},{5,7},{6,4},{7,5},{8,10},{9,11},{10,... | collective-permute-start | bytes 589832 | tf_op jit(solution)/shard_map/ppermute | solution.py:901
  (105 other events, 722.7 us)
